TPU v7x, 32 devices: a whole 2x2x4 slice. The times are simulated.
32 devices in a mesh: expert: 4 (over y, x), head: 8 (over z, core).
Axes of the slice: x: 2, y: 2, z: 4, core: 2. Of those that a mesh axis runs over, the one named last changes fastest.
Arguments:
- table_cells: bfloat16 [2048, 2, 2048], P(('expert', 'head')), may hold values from -8 to 8
- w_query: bfloat16 [2048, 2048], P(None, 'head')
- w_key: bfloat16 [2048, 2048], P(None, 'head')
- w_value: bfloat16 [2048, 2048], P(None, 'head'), may hold values from -0.125 to 0.125
- w_out: bfloat16 [2048, 2048], P('head'), may hold values from -0.125 to 0.125
- norm_gain: bfloat16 [2048], replicated, may hold values from 0.099609375 to 1.8984375
- w_gate: bfloat16 [32, 704, 2048], P(('expert', 'head')), may hold values from -0.125 to 0.125
- w_up: bfloat16 [32, 704, 2048], P(('expert', 'head')), may hold values from -0.125 to 0.125
- w_down: bfloat16 [32, 704, 2048], P(('expert', 'head')), may hold values from -0.15625 to 0.15625
- lengths: int32 [2], replicated, may hold values from 512 to 2048, as said below
- expert_of_cell: int32 [2048, 2], P(('expert', 'head')), may hold values from 0 to 15, as said below
- slot_of_cell: int32 [2048, 2], P(('expert', 'head')), may hold values from 0 to 15, as said below
Outputs:
- updated_cells: bfloat16 [2048, 2, 2048], P(('expert', 'head'))
Inputs may be any that keep to these rules, and one draw needn't show every extreme that they name: `lengths`: one table in every draw has all 2048 cells. `expert_of_cell`: within the 128 cells of one device (aligned blocks in row-major order), no expert has more than 16 cells, and in every draw one expert has exactly 16 cells in every device's block. `slot_of_cell`: cells of one device with the same expert have distinct slots.
All inputs are finite; a program needn't handle non-finite values.
Results may differ from a plain program's by a relative error of at most 0.014.
Values may be sent and summed in bfloat16 or wider, within the bound.
No kernel may reach another device: no remote copies, remote signals or barrier semaphores. Data moves between devices by JAX's collectives and lax.ppermute only.
A program may use at most 128 MiB of HBM per device.

v0:
```python
import math

import jax
import jax.numpy as jnp
from jax import lax
from jax.sharding import PartitionSpec as P

DH = 128


def from_partner(block, axis, bit):
    count = lax.axis_size(axis)
    route = []
    for low in range(count):
        high = low | 1 << bit
        if high != low and high < count:
            route += [(low, high), (high, low)]
    return lax.ppermute(block, axis, route)


def expert_half(slot_rows, gate_half, up_half, down_half):
    contract_rows = (((1,), (1,)), ((), ()))
    gate_t = lax.dot_general(
        gate_half, slot_rows, contract_rows, preferred_element_type=jnp.float32
    )
    up_t = lax.dot_general(up_half, slot_rows, contract_rows, preferred_element_type=jnp.float32)
    hidden = (jax.nn.silu(gate_t) * up_t).astype(jnp.bfloat16)
    product = lax.dot_general(
        hidden, down_half, (((0,), (0,)), ((), ())), preferred_element_type=jnp.float32
    )
    return product.astype(jnp.bfloat16)


def shards(
    table_cells,
    w_query,
    w_key,
    w_value,
    w_out,
    norm_gain,
    w_gate,
    w_up,
    w_down,
    lengths,
    expert_of_cell,
    slot_of_cell,
):
    cell_count, tables, model_width = table_cells.shape
    head_width = w_query.shape[1]
    head_count = head_width // DH
    score_scale = 1.0 / math.sqrt(DH)
    joined = jnp.concatenate([w_query, w_key, w_value], axis=1)
    shard_rows = lax.all_gather(table_cells, "head", axis=0, tiled=True)
    rows_here = shard_rows.shape[0]
    mixed_rows = jnp.dot(
        shard_rows.reshape(rows_here * tables, model_width),
        joined,
        preferred_element_type=jnp.float32,
    )
    projected = mixed_rows.astype(jnp.bfloat16).reshape(rows_here, tables, 3 * head_width)
    row_cells = projected.shape[0]
    queries = projected[:, :, :head_width].reshape(row_cells, tables, head_count, DH)
    key_rows = projected[:, :, head_width : 2 * head_width]
    value_rows = projected[:, :, 2 * head_width :]
    offset = lax.axis_index("expert") * row_cells
    own_positions = offset + jnp.arange(row_cells, dtype=jnp.int32)
    start_state = (
        jnp.full((tables, head_count, row_cells), -1e30, jnp.float32),
        jnp.zeros((tables, head_count, row_cells), jnp.float32),
        jnp.zeros((tables, head_count, row_cells, DH), jnp.float32),
    )
    key_piece = lax.all_gather(key_rows, "expert", axis=0, tiled=True)
    value_piece = lax.all_gather(value_rows, "expert", axis=0, tiled=True)
    piece_len = key_piece.shape[0]
    block_len = math.gcd(piece_len, 512)
    block_count = piece_len // block_len
    key_blocks = key_piece.reshape(block_count, block_len, tables, head_count, DH)
    value_blocks = value_piece.reshape(block_count, block_len, tables, head_count, DH)
    block_starts = jnp.arange(block_count, dtype=jnp.int32) * block_len

    def step(carried, block_item):
        running_max, running_sum, accum = carried
        key_block, value_block, block_first = block_item
        scores = (
            jnp.einsum("qshd,kshd->shqk", queries, key_block, preferred_element_type=jnp.float32)
            * score_scale
        )
        key_valid = (block_first + jnp.arange(block_len, dtype=jnp.int32))[None, :] < lengths[
            :, None
        ]
        scores = jnp.where(key_valid[:, None, None, :], scores, -jnp.inf)
        new_max = jnp.maximum(running_max, jnp.max(scores, axis=-1))
        factor = jnp.exp(running_max - new_max)
        exp_scores = jnp.exp(scores - new_max[..., None])
        running_sum = running_sum * factor + jnp.sum(exp_scores, axis=-1)
        accum = accum * factor[..., None] + jnp.einsum(
            "shqk,kshd->shqd",
            exp_scores.astype(jnp.bfloat16),
            value_block,
            preferred_element_type=jnp.float32,
        )
        return ((new_max, running_sum, accum), None)

    finished, _ = lax.scan(step, start_state, (key_blocks, value_blocks, block_starts))
    running_max, running_sum, accum = finished
    normalized = accum / running_sum[..., None]
    live = own_positions[None, :] < lengths[:, None]
    normalized = jnp.where(live[:, None, :, None], normalized, 0.0)
    attended = (
        jnp.transpose(normalized, (2, 0, 1, 3))
        .reshape(row_cells, tables, head_width)
        .astype(jnp.bfloat16)
    )
    count_rows = cell_count * lax.axis_size("head")
    product = jnp.dot(
        attended.reshape(count_rows * tables, head_width), w_out, preferred_element_type=jnp.float32
    )
    summed = lax.psum_scatter(
        product.reshape(count_rows, tables, model_width).astype(jnp.bfloat16),
        "head",
        scatter_dimension=0,
        tiled=True,
    ).astype(jnp.float32)
    residual = table_cells.astype(jnp.float32) + summed
    mean_square = jnp.mean(residual * residual, axis=-1, keepdims=True)
    normed = (residual * lax.rsqrt(mean_square + 1e-06) * norm_gain.astype(jnp.float32)).astype(
        jnp.bfloat16
    )
    rows_dev = cell_count * tables
    normed_rows = normed.reshape(rows_dev, model_width)
    expert_count = lax.axis_size("expert") * lax.axis_size("head") // 2
    slot_cap = 2 * max(1, rows_dev // expert_count)
    target = expert_of_cell.reshape(rows_dev) * slot_cap + slot_of_cell.reshape(rows_dev)
    slot_table = (
        jnp.arange(expert_count * slot_cap, dtype=jnp.int32)[:, None] == target[None, :]
    ).astype(jnp.bfloat16)
    send_rows = jnp.dot(slot_table, normed_rows, preferred_element_type=jnp.float32).astype(
        jnp.bfloat16
    )
    gate_half = w_gate[0]
    up_half = w_up[0]
    down_half = w_down[0]
    split_rows = send_rows.reshape(2 * expert_count, slot_cap // 2, model_width)
    received = lax.all_to_all(
        split_rows, ("expert", "head"), split_axis=0, concat_axis=0, tiled=True
    )
    item_count = received.shape[1]
    partner_rows = from_partner(received, "head", 0)
    apply_received = jnp.concatenate([received, partner_rows], axis=1)
    sources = apply_received.shape[0]
    apply_item_count = apply_received.shape[1]
    flat_rows = apply_received.reshape(sources * apply_item_count, model_width)
    computed = expert_half(flat_rows, gate_half, up_half, down_half).reshape(
        sources, apply_item_count, model_width
    )
    returned = from_partner(computed[:, item_count:], "head", 0)
    merged = (computed[:, :item_count].astype(jnp.float32) + returned.astype(jnp.float32)).astype(
        jnp.bfloat16
    )
    gathered = lax.all_to_all(merged, ("expert", "head"), split_axis=0, concat_axis=0, tiled=True)
    combined = gathered.reshape(expert_count * slot_cap, model_width)
    expert_out = lax.dot_general(
        slot_table, combined, (((0,), (0,)), ((), ())), preferred_element_type=jnp.float32
    )
    updated = (residual.reshape(rows_dev, model_width) + expert_out).astype(jnp.bfloat16)
    return updated.reshape(cell_count, tables, model_width)


def solution(mesh):
    placed = (
        P(("expert", "head"), None, None),
        P(None, "head"),
        P(None, "head"),
        P(None, "head"),
        P("head", None),
        P(),
        P(("expert", "head"), None, None),
        P(("expert", "head"), None, None),
        P(("expert", "head"), None, None),
        P(),
        P(("expert", "head"), None),
        P(("expert", "head"), None),
    )
    return jax.shard_map(
        shards,
        mesh=mesh,
        in_specs=placed,
        out_specs=P(("expert", "head"), None, None),
        check_vma=False,
    )
```

profile of v0, /device:TPU:0, one launch (start us, length us, event | category | flops | bytes accessed | tf_op | source)
XLA Modules:
  0.0 376.5 jit_solution(4066280734883950800)
XLA Ops:
  7.3 51.5 %all-gather.4.cloned.1.call-done = bf16[512,2,2048]{2,1,0:T(2,128)(2,1)} async-done(((bf16[64,2,2048]{2,1,0:T(2,128)(2,1)}), bf16[512,2,2048]{2,1,0:T(2,128)(2,1)}) %all-gather.4.cloned.1.call-update) | async-done | bytes 4194320 | tf_op jit(solution)/shard_map/all_gather | solution.py:53
  58.8 7.2 %reshape.127 = bf16[1024,2048]{1,0:T(8,128)(2,1)} reshape(bf16[512,2,2048]{2,1,0:T(2,128)(2,1)} %all-gather.4.cloned.1.call-done) | data formatting | bytes 8388608 | tf_op jit(solution)/shard_map/reshape | solution.py:56
  66.0 7.8 %fusion.33 = bf16[1024,768]{0,1:T(8,128)(2,1)} fusion(bf16[1024,2048]{1,0:T(8,128)(2,1)} %reshape.127, bf16[2048,256]{1,0:T(8,128)(2,1)} %param.17, bf16[2048,256]{1,0:T(8,128)(2,1)} %param.16, bf16[2048,256]{1,0:T(8,128)(2,1)} %param.15), kind=kOutput, calls=%fused_computation.47 | convolution fusion | flops 3231449088 | bytes 8912896 | tf_op jit(solution)/shard_map/dot_general | solution.py:55
  76.5 4.5 %reshape.128 = bf16[512,2,768]{2,1,0:T(2,128)(2,1)} reshape(bf16[1024,768]{1,0:T(8,128)(2,1)} %copy.32) | data formatting | bytes 3145728 | tf_op jit(solution)/shard_map/reshape | solution.py:60
  81.0 3.4 fusion.53
  88.3 30.3 %all-gather.6.cloned.1.call-done = bf16[2048,2,256]{2,1,0:T(2,128)(2,1)} async-done(((bf16[512,2,256]{2,1,0:T(2,128)(2,1)}), bf16[2048,2,256]{2,1,0:T(2,128)(2,1)}) %all-gather.6.cloned.1.call-update) | async-done | bytes 2097168 | tf_op jit(solution)/shard_map/all_gather | solution.py:72
  118.6 6.8 %reshape.140 = bf16[4,512,2,2,128]{4,3,2,1,0:T(2,128)(2,1)} reshape(bf16[2048,2,256]{2,1,0:T(2,128)(2,1)} %all-gather.6.cloned.1.call-done) | data formatting | bytes 4194304 | tf_op jit(solution)/shard_map/reshape | solution.py:77
  125.3 30.4 %all-gather.8.cloned.1.call-done = bf16[2048,2,256]{2,1,0:T(2,128)(2,1)} async-done(((bf16[512,2,256]{2,1,0:T(2,128)(2,1)}), bf16[2048,2,256]{2,1,0:T(2,128)(2,1)}) %all-gather.8.cloned.1.call-update) | async-done | bytes 2097168 | tf_op jit(solution)/shard_map/all_gather | solution.py:73
  155.8 6.8 %reshape.141 = bf16[4,512,2,2,128]{4,3,2,1,0:T(2,128)(2,1)} reshape(bf16[2048,2,256]{2,1,0:T(2,128)(2,1)} %all-gather.8.cloned.1.call-done) | data formatting | bytes 4194304 | tf_op jit(solution)/shard_map/reshape | solution.py:78
  162.6 56.7 %while.15 = (s32[]{:T(128)}, f32[2,2,512]{2,1,0:T(2,128)S(1)}, f32[2,2,512]{2,1,0:T(2,128)S(1)}, f32[2,2,512,128]{3,2,1,0:T(8,128)}, s32[4]{0:T(128)S(1)}, /*ind...) while((s32[]{:T(128)}, f32[2,2,512]{2,1,0:T(2,128)S(1)}, ...), condition=%wide.region_3.4_spmd.clone, body=%wide.region_0.3_spmd.clone.sunk | while | flops 549203456 | bytes 35266736 | solution.py:104
  169.3 3.3 fusion.69
  172.7 3.8 fusion.71
  183.2 3.3 fusion.69
  186.6 4.1 %fusion.71 = f32[2,2,512,128]{3,2,1,0:T(8,128)} fusion(f32[2,2,512,512]{3,2,1,0:T(8,128)S(1)} %copy-done.1, f32[2,2,512]{2,1,0:T(2,128)S(1)} %fusion.68, pred[2,512]{1,0:T(4,128)(4,1)S(1)} %broadcast_compare_fusion.3, f32[2,2,512,128]{3,2,1,0:T(8,128)} %get-tuple-element.213, bf16[1,512,2,2,128]{4,3,2,1,0:T(2,128)(2,1)} %get-tuple-element.197, ...), kind=kOutput, calls=%fused_computation.11.clone.1 | convolution fusion | flops 273416192 | bytes 6833153 | tf_op jit(solution)/shard_map/while/body/eval_jaxpr/shqk,kshd->shqd/dot_general | solution.py:96
  197.5 3.3 fusion.69
  200.9 4.1 %fusion.71 = f32[2,2,512,128]{3,2,1,0:T(8,128)} fusion(f32[2,2,512,512]{3,2,1,0:T(8,128)S(1)} %copy-done.1, f32[2,2,512]{2,1,0:T(2,128)S(1)} %fusion.68, pred[2,512]{1,0:T(4,128)(4,1)S(1)} %broadcast_compare_fusion.3, f32[2,2,512,128]{3,2,1,0:T(8,128)} %get-tuple-element.213, bf16[1,512,2,2,128]{4,3,2,1,0:T(2,128)(2,1)} %get-tuple-element.197, ...), kind=kOutput, calls=%fused_computation.11.clone.1 | convolution fusion | flops 273416192 | bytes 6833153 | tf_op jit(solution)/shard_map/while/body/eval_jaxpr/shqk,kshd->shqd/dot_general | solution.py:96
  211.7 3.3 fusion.69
  215.1 4.1 %fusion.71 = f32[2,2,512,128]{3,2,1,0:T(8,128)} fusion(f32[2,2,512,512]{3,2,1,0:T(8,128)S(1)} %copy-done.1, f32[2,2,512]{2,1,0:T(2,128)S(1)} %fusion.68, pred[2,512]{1,0:T(4,128)(4,1)S(1)} %broadcast_compare_fusion.3, f32[2,2,512,128]{3,2,1,0:T(8,128)} %get-tuple-element.213, bf16[1,512,2,2,128]{4,3,2,1,0:T(2,128)(2,1)} %get-tuple-element.197, ...), kind=kOutput, calls=%fused_computation.11.clone.1 | convolution fusion | flops 273416192 | bytes 6833153 | tf_op jit(solution)/shard_map/while/body/eval_jaxpr/shqk,kshd->shqd/dot_general | solution.py:96
  223.2 4.5 %convolution_convert_fusion = bf16[512,2,2048]{2,0,1:T(8,128)(2,1)} fusion(bf16[512,2,256]{0,2,1:T(8,128)(2,1)S(1)} %bitcast.87, bf16[256,2048]{1,0:T(8,128)(2,1)} %param.18), kind=kOutput, calls=%fused_computation.27 | convolution fusion | flops 1075838976 | bytes 5767168 | tf_op jit(solution)/shard_map/dot_general | solution.py:115
  228.6 49.2 %reduce-scatter.2.cloned.1.call-done = bf16[64,2,2048]{2,0,1:T(8,128)(2,1)} async-done(((bf16[512,2,2048]{2,0,1:T(8,128)(2,1)}), bf16[64,2,2048]{2,0,1:T(8,128)(2,1)}) %reduce-scatter.2.cloned.1.call-update) | async-done | bytes 524304 | tf_op jit(solution)/shard_map/reduce_scatter | solution.py:118
  284.5 30.1 %all_to_all.10 = bf16[32,8,2048]{2,1,0:T(8,128)(2,1)S(1)} all-to-all(bf16[32,8,2048]{2,1,0:T(8,128)(2,1)S(1)} %fusion.28), channel_id=1, replica_groups=mesh['expert'=4,'head'=8] {'expert','head'}, dimensions={0} | all-to-all | bytes 2097152 | tf_op jit(solution)/shard_map/all_to_all | solution.py:144
  321.7 7.7 %convolution_convert_fusion.1 = bf16[512,2048]{1,0:T(8,128)(2,1)} fusion(bf16[1,704,2048]{2,1,0:T(8,128)(2,1)S(1)} %copy-done, f32[704,512]{1,0:T(8,128)} %fusion.36, bf16[512,2048]{1,0:T(8,128)(2,1)} %bitcast.85, bf16[1,704,2048]{2,1,0:T(8,128)(2,1)} %param.21), kind=kOutput, calls=%fused_computation.34 | convolution fusion | flops 2956001280 | bytes 11403264 | tf_op jit(solution)/shard_map/dot_general | solution.py:28
  336.0 3.4 all-to-all-start.1
  345.3 21.6 %all-to-all-done.1 = bf16[32,8,2048]{2,1,0:T(8,128)(2,1)} async-done(((bf16[32,8,2048]{2,1,0:T(8,128)(2,1)}), bf16[32,8,2048]{2,1,0:T(8,128)(2,1)}, u32[]{:S(2)}, u32[]{:S(2)}) %all-to-all-start.1) | async-done | bytes 1048608 | tf_op jit(solution)/shard_map/all_to_all | solution.py:160
  (97 shorter events, 68.8 us)
Async XLA Ops:
  6.5 315.2 %copy-start = (bf16[1,704,2048]{2,1,0:T(8,128)(2,1)S(1)}, bf16[1,704,2048]{2,1,0:T(8,128)(2,1)}, u32[]{:S(2)}) copy-start(bf16[1,704,2048]{2,1,0:T(8,128)(2,1)} %param.22) | copy-start | bytes 8650756
  6.5 52.3 %all-gather.4.cloned.1.call-start = ((), (), s32[]{:S(2)}) async-start(), calls=%async_computation.3 | async-start | bytes 4718592 | tf_op jit(solution)/shard_map/all_gather | solution.py:53
  7.3 111.3 %all-gather.6.cloned.1.call-start = ((), (), s32[]{:S(2)}) async-start(), calls=%async_computation.4 | async-start | bytes 2621440 | tf_op jit(solution)/shard_map/all_gather | solution.py:72
  81.0 4.5 %copy-start.4 = (s32[2]{0:T(128)S(1)}, s32[2]{0:T(128)}, u32[]{:S(2)}) copy-start(s32[2]{0:T(128)} %param.23) | copy-start | bytes 28
  84.4 71.4 %all-gather.8.cloned.1.call-start = ((), (), s32[]{:S(2)}) async-start(), calls=%async_computation.5 | async-start | bytes 2621440 | tf_op jit(solution)/shard_map/all_gather | solution.py:73
  85.1 192.7 %reduce-scatter.2.cloned.1.call-start = ((), (), s32[]{:S(2)}) async-start(), calls=%async_computation.6 | async-start | bytes 4718592 | tf_op jit(solution)/shard_map/reduce_scatter | solution.py:118
  169.3 3.4 copy-start.1
  183.2 3.4 copy-start.1
  197.4 3.4 copy-start.1
  211.7 3.4 copy-start.1
  227.6 0.7 copy-start.5
  227.6 0.7 copy-start.6
  227.6 0.7 copy-start.7
  227.6 50.2 %copy-start.2 = (bf16[64,2,2048]{2,1,0:T(2,128)(2,1)S(1)}, bf16[64,2,2048]{2,1,0:T(2,128)(2,1)}, u32[]{:S(2)}) copy-start(bf16[64,2,2048]{2,1,0:T(2,128)(2,1)} %param.14) | copy-start | bytes 1572868
  284.5 34.4 %copy-start.8 = (bf16[1,704,2048]{2,1,0:T(8,128)(2,1)S(1)}, bf16[1,704,2048]{2,1,0:T(8,128)(2,1)}, u32[]{:S(2)}) copy-start(bf16[1,704,2048]{2,1,0:T(8,128)(2,1)} %param.20) | copy-start | bytes 8650756
  314.7 2.7 collective-permute-start
  317.6 1.3 copy-start.3
  330.6 2.7 collective-permute-start.1
  336.0 31.0 %all-to-all-start.1 = ((bf16[32,8,2048]{2,1,0:T(8,128)(2,1)}), bf16[32,8,2048]{2,1,0:T(8,128)(2,1)}, u32[]{:S(2)}, u32[]{:S(2)}) async-start(bf16[32,8,2048]{2,1,0:T(8,128)(2,1)} %add_convert_fusion), calls=%async_computation.2 | async-start | bytes 2097152 | tf_op jit(solution)/shard_map/all_to_all | solution.py:160
Sparse Core Ops, SparseCore 0:
  9.0 49.8 all-gather.3
  84.5 34.0 all-gather.5
  120.4 35.2 all-gather.7
  227.8 49.9 reduce-scatter.1
where the time goes:
time: 378 us; the launch traced here: 376 us
  waiting for transfers between devices  190 us (50%)
  local copies, waits for them, and re-layouts  62.5 us (17%)
  matrix products  52.9 us (14%)
  blocking collectives  30.1 us (8%)
  other arithmetic  24 us (6%)
  between operations  13.3 us (4%)
  starting transfers between devices  3.89 us (1%)
    all_gather x1, waiting for transfers between devices, shards(): shard_rows = lax.all_gather(table_cells, 'head', axis=0, tiled=True)  51.5 us
    reduce_scatter x1, waiting for transfers between devices, shards(): lax.psum_scatter(product.reshape(count_rows, tables, model_width).astype(...  49.2 us
    all_gather x1, waiting for transfers between devices, shards(): value_piece = lax.all_gather(value_rows, 'expert', axis=0, tiled=True)  30.4 us
    all_gather x1, waiting for transfers between devices, shards(): key_piece = lax.all_gather(key_rows, 'expert', axis=0, tiled=True)  30.3 us
    all_to_all x1, blocking collectives, shards(): lax.all_to_all(split_rows, ('expert', 'head'), split_axis=0, concat_axis=...  30.1 us
    all_to_all x1, waiting for transfers between devices, shards(): lax.all_to_all(merged, ('expert', 'head'), split_axis=0, concat_axis=0, t...  21.6 us
    dot_general x4, matrix products, step(): jnp.einsum('shqk,kshd->shqd', exp_scores.astype(jnp.bfloat16), value_bloc...  16 us
    dynamic_slice x8, local copies, waits for them, and re-layouts, shards(): lax.scan(step, start_state, (key_blocks, value_blocks, block_starts))  13.2 us
  transfers between devices with their start and end apart: 7, of which 7 were waited for; matrix products, arithmetic and copies ran while one was open for 4% of the time, Pallas kernels for 0%

commit v1 on v0

--- a/solution.py
+++ b/solution.py
@@ -1,11 +1,339 @@
+import functools
 import math
 
 import jax
 import jax.numpy as jnp
 from jax import lax
+from jax.experimental import pallas as pl
+from jax.experimental.pallas import tpu as pltpu
 from jax.sharding import PartitionSpec as P
 
 DH = 128
+VMEM = pl.BlockSpec(memory_space=pltpu.VMEM)
+SMEM = pl.BlockSpec(memory_space=pltpu.SMEM)
+ROWS_BY_ROWS = (((1,), (1,)), ((), ()))
+GRANT = 56 * 1024 * 1024
+
+
+def local_call(body, outs, args, specs, flops, scratch=()):
+    moved = sum(a.size * a.dtype.itemsize for a in list(args) + list(outs))
+    return pl.pallas_call(
+        body,
+        out_shape=outs,
+        in_specs=specs,
+        out_specs=[VMEM] * len(outs),
+        scratch_shapes=list(scratch),
+        compiler_params=pltpu.CompilerParams(vmem_limit_bytes=GRANT),
+        cost_estimate=pl.CostEstimate(flops=flops, bytes_accessed=moved, transcendentals=0),
+    )(*args)
+
+
+def shape_of(dims, dtype=jnp.bfloat16):
+    return jax.ShapeDtypeStruct(dims, dtype)
+
+
+def swap_cores(block):
+    count = lax.axis_size("head")
+    return lax.ppermute(block, "head", [(h, h ^ 1) for h in range(count)])
+
+
+def along_z(block, step, first):
+    planes = lax.axis_size("head") // 2
+    route = []
+    for z in range(planes):
+        there = z + step
+        behind = z if step > 0 else planes - 1 - z
+        if 0 <= there < planes and behind >= first:
+            route += [(2 * z + core, 2 * there + core) for core in range(2)]
+    return lax.ppermute(block, "head", route)
+
+
+def round_z(block, step):
+    count = lax.axis_size("head")
+    return lax.ppermute(block, "head", [(h, (h - 2 * step) % count) for h in range(count)])
+
+
+def in_plane(block, bits):
+    count = lax.axis_size("expert")
+    return lax.ppermute(block, "expert", [(e, e ^ bits) for e in range(count)])
+
+
+def in_plane_and_core(block, bits, core_bit):
+    heads = lax.axis_size("head")
+    count = lax.axis_size("expert") * heads
+    route = [(d, ((d // heads) ^ bits) * heads + ((d % heads) ^ core_bit)) for d in range(count)]
+    return lax.ppermute(block, ("expert", "head"), route)
+
+
+def project_body(pieces, half, *refs):
+    inputs, weight_ref, outs = refs[: 4 * pieces], refs[4 * pieces], refs[4 * pieces + 1 :]
+    width = weight_ref.shape[1] // 2
+    for table in range(2):
+        for piece in range(pieces):
+            first, second = inputs[4 * piece + 2 * table : 4 * piece + 2 * table + 2]
+            rows = jnp.concatenate([first[...], second[...]], axis=0)
+            mixed = jnp.dot(rows, weight_ref[...], preferred_element_type=jnp.float32)
+            mixed = mixed.astype(jnp.bfloat16)
+            span = pl.ds(piece * 2 * half, 2 * half)
+            outs[2 * table][span, :] = mixed[:, :width]
+            outs[2 * table + 1][span, :] = mixed[:, width:]
+
+
+def project(groups, weight):
+    pieces, half, width = len(groups), groups[0][0].shape[0], weight.shape[1] // 2
+    args = [block for group in groups for block in group] + [weight]
+    outs = [shape_of((pieces * 2 * half, width))] * 4
+    return local_call(
+        functools.partial(project_body, pieces, half),
+        outs,
+        args,
+        [VMEM] * len(args),
+        2 * pieces * 4 * half * weight.size,
+    )
+
+
+def attend_body(block, place_ref, bias_ref, *refs):
+    sources = 4
+    early, middle, late = refs[:4], refs[4:8], refs[8:12]
+    outs, (queries, keys, values) = refs[12:16], refs[16:19]
+    place = place_ref[0]
+    for source in range(sources):
+        last = late[source][...]
+        near = early[source][pl.ds(block, block), :]
+        far = early[source][pl.ds(2 * block, block), :]
+        rows = (
+            early[source][pl.ds(0, block), :],
+            jnp.where(place == 0, last, near),
+            middle[source][...],
+            jnp.where(place == 3, last, far),
+        )
+        for offset in range(4):
+            key_span = pl.ds((offset * sources + source) * block, block)
+            queries[key_span, :] = rows[offset][:, :DH]
+            keys[key_span, :] = rows[offset][:, DH : 2 * DH]
+            values[key_span, :] = rows[offset][:, 2 * DH :]
+    scale = 1.0 / math.sqrt(DH) * math.log2(math.e)
+    chunk = 256
+    per_out = sources * block // chunk
+    for step in range(4 * per_out):
+        scores = lax.dot_general(
+            queries[pl.ds(step * chunk, chunk), :],
+            keys[...],
+            ROWS_BY_ROWS,
+            preferred_element_type=jnp.float32,
+        )
+        scores = scores + bias_ref[...]
+        top = jnp.max(scores, axis=1, keepdims=True)
+        weights = jnp.exp2((scores - top) * scale)
+        total = jnp.sum(weights, axis=1, keepdims=True)
+        mixed = jnp.dot(
+            weights.astype(jnp.bfloat16), values[...], preferred_element_type=jnp.float32
+        )
+        outs[step // per_out][pl.ds(step % per_out * chunk, chunk), :] = (mixed / total).astype(
+            jnp.bfloat16
+        )
+
+
+def regroup_body(block, *refs):
+    for offset in range(4):
+        for target in range(8):
+            refs[4 + target][pl.ds(offset * block, block), :] = refs[offset][
+                pl.ds(target * block, block), :
+            ]
+
+
+def join_body(planes, place_ref, own_ref, live_ref, target_ref, gain_ref, *refs):
+    pieces, out_weight = refs[:8], refs[8]
+    residual_ref, send_ref, joined = refs[9:]
+    place, core, parity = place_ref[0], place_ref[1], place_ref[2]
+    block = joined.shape[0] // 2
+    for source in range(4):
+        table, head_bit = source >> 1, source & 1
+        for core_bit in range(2):
+            piece = pieces[2 * source + core_bit]
+            for offset in range(planes):
+                device = 2 * lax.rem(place + offset, planes) + (core ^ core_bit)
+                head = 2 * device + (parity ^ head_bit)
+                columns = pl.ds(pl.multiple_of(head * DH, DH), DH)
+                joined[pl.ds(table * block, block), columns] = piece[
+                    pl.ds(offset * block, block), :
+                ]
+    attended = jnp.where(live_ref[...] > 0, joined[...].astype(jnp.float32), 0.0)
+    summed = jnp.dot(
+        attended.astype(jnp.bfloat16), out_weight[...], preferred_element_type=jnp.float32
+    )
+    residual = own_ref[...].astype(jnp.float32) + summed
+    residual_ref[...] = residual
+    mean_square = jnp.mean(residual * residual, axis=1, keepdims=True)
+    normed = residual * lax.rsqrt(mean_square + 1e-06) * gain_ref[...].astype(jnp.float32)
+    slots = send_ref.shape[0]
+    table = lax.broadcasted_iota(jnp.int32, (slots, joined.shape[0]), 0) == target_ref[...]
+    send_ref[...] = jnp.dot(
+        table.astype(jnp.float32).astype(jnp.bfloat16),
+        normed.astype(jnp.bfloat16),
+        preferred_element_type=jnp.float32,
+    ).astype(jnp.bfloat16)
+
+
+def expert_body(own_ref, other_ref, gate_ref, up_ref, down_ref, own_out, other_out):
+    for rows_ref, out_ref in ((other_ref, other_out), (own_ref, own_out)):
+        rows = rows_ref[...]
+        gate = lax.dot_general(
+            rows, gate_ref[...], ROWS_BY_ROWS, preferred_element_type=jnp.float32
+        )
+        up = lax.dot_general(rows, up_ref[...], ROWS_BY_ROWS, preferred_element_type=jnp.float32)
+        hidden = (gate / (1.0 + jnp.exp(-gate)) * up).astype(jnp.bfloat16)
+        out_ref[...] = jnp.dot(
+            hidden, down_ref[...], preferred_element_type=jnp.float32
+        ).astype(jnp.bfloat16)
+
+
+def paired_shards(
+    table_cells,
+    w_query,
+    w_key,
+    w_value,
+    w_out,
+    norm_gain,
+    w_gate,
+    w_up,
+    w_down,
+    lengths,
+    expert_of_cell,
+    slot_of_cell,
+):
+    cells, tables, width = table_cells.shape
+    heads = lax.axis_size("head")
+    planes = heads // 2
+    spot, place_head = lax.axis_index("expert"), lax.axis_index("head")
+    mine, parity = spot // 2, spot % 2
+    place, core = place_head // 2, place_head % 2
+
+    by_table = jnp.transpose(table_cells, (1, 0, 2))
+    by_table = jnp.where(mine == 0, by_table, by_table[::-1])
+    own = [by_table[0], by_table[1]]
+
+    def columns(which):
+        return [
+            lax.dynamic_slice_in_dim(w, which * DH, DH, 1) for w in (w_query, w_key, w_value)
+        ]
+
+    weight = jnp.concatenate(columns(parity) + columns(1 - parity), axis=1)
+
+    up = [[block] for block in own]
+    down = [[block] for block in own]
+    for stage in range(planes - 1):
+        for table in range(2):
+            up[table].append(along_z(up[table][stage], 1, stage))
+            down[table].append(along_z(down[table][stage], -1, stage))
+
+    def with_other(blocks):
+        return [part for block in blocks for part in (block, swap_cores(block))]
+
+    later = [jnp.where(place < 2, down[t][2], up[t][2]) for t in range(2)]
+    last = [jnp.where(place < 2, down[t][3], up[t][3]) for t in range(2)]
+    early_out = project(
+        [
+            with_other(own),
+            with_other([up[0][1], up[1][1]]),
+            with_other([down[0][1], down[1][1]]),
+        ],
+        weight,
+    )
+    middle_out = project([with_other(later)], weight)
+    late_out = project([with_other(last)], weight)
+
+    def spread(outs):
+        return [outs[0]] + [in_plane(outs[bits], bits) for bits in range(1, 4)]
+
+    shared = spread(early_out) + spread(middle_out) + spread(late_out)
+
+    block = 2 * cells
+    offsets = jnp.arange(planes, dtype=jnp.int32)[:, None, None, None]
+    sources = jnp.arange(4, dtype=jnp.int32)[None, :, None, None]
+    sides = jnp.arange(2, dtype=jnp.int32)[None, None, :, None]
+    inner = jnp.arange(cells, dtype=jnp.int32)[None, None, None, :]
+    device = (spot ^ sources) * heads + 2 * ((place - offsets) % planes) + (core ^ sides)
+    positions = (device * cells + inner).reshape(1, planes * 4 * block)
+    bias = jnp.where(positions < lengths[mine], 0.0, -jnp.inf).astype(jnp.float32)
+    count = planes * 4 * block
+    attended = local_call(
+        functools.partial(attend_body, block),
+        [shape_of((4 * block, DH))] * 4,
+        [place.reshape(1).astype(jnp.int32), bias] + shared,
+        [SMEM] + [VMEM] * 13,
+        4 * count * count * DH,
+        [pltpu.VMEM((count, DH), jnp.bfloat16)] * 3,
+    )
+    arrived = [attended[0]] + [round_z(attended[k], k) for k in range(1, planes)]
+    grouped = local_call(
+        functools.partial(regroup_body, cells),
+        [shape_of((planes * cells, DH))] * 8,
+        arrived,
+        [VMEM] * 4,
+        0,
+    )
+    pieces = [grouped[0]] + [
+        in_plane_and_core(grouped[i], i >> 1, i & 1) for i in range(1, 8)
+    ]
+
+    quarter = w_out.shape[0] // 4
+    part = lax.dynamic_slice_in_dim(w_out, spot * quarter, quarter, 0)
+    parts = lax.all_gather(part, "head", axis=0, tiled=False)
+    whole = lax.all_gather(parts, "expert", axis=1, tiled=False)
+    out_weight = whole.reshape(heads * w_out.shape[0], width)
+
+    rows_dev = cells * tables
+    own_rows = by_table.reshape(rows_dev, width)
+    own_positions = (spot * heads + place_head) * cells + jnp.arange(cells, dtype=jnp.int32)
+    table_order = jnp.stack([mine, 1 - mine])
+    live = (own_positions[None, :] < lengths[table_order][:, None]).astype(jnp.int32)
+    expert_count = lax.axis_size("expert") * heads // 2
+    slot_cap = 2 * max(1, rows_dev // expert_count)
+    target = expert_of_cell * slot_cap + slot_of_cell
+    target = jnp.take(target.T, table_order, axis=0).reshape(1, rows_dev)
+    slots = expert_count * slot_cap
+    residual, send_rows = local_call(
+        functools.partial(join_body, planes),
+        [shape_of((rows_dev, width), jnp.float32), shape_of((slots, width))],
+        [
+            jnp.stack([place, core, parity]).astype(jnp.int32),
+            own_rows,
+            live.reshape(rows_dev, 1),
+            target,
+            norm_gain.reshape(1, width),
+        ]
+        + pieces
+        + [out_weight],
+        [SMEM] + [VMEM] * 13,
+        2 * rows_dev * width * (width + slots),
+        [pltpu.VMEM((rows_dev, width), jnp.bfloat16)],
+    )
+
+    everyone = ("expert", "head")
+    received = lax.all_to_all(
+        send_rows.reshape(2 * expert_count, slot_cap // 2, width), everyone, 0, 0, tiled=True
+    ).reshape(slots, width)
+    other_rows = swap_cores(received)
+    own_part, other_part = local_call(
+        expert_body,
+        [shape_of((slots, width))] * 2,
+        [received, other_rows, w_gate[0], w_up[0], w_down[0]],
+        [VMEM] * 5,
+        2 * 2 * slots * 3 * w_gate.size,
+    )
+    returned = swap_cores(other_part)
+    merged = (own_part.astype(jnp.float32) + returned.astype(jnp.float32)).astype(jnp.bfloat16)
+    gathered = lax.all_to_all(
+        merged.reshape(2 * expert_count, slot_cap // 2, width), everyone, 0, 0, tiled=True
+    ).reshape(slots, width)
+    chosen = (jnp.arange(slots, dtype=jnp.int32)[:, None] == target).astype(jnp.bfloat16)
+    expert_out = lax.dot_general(
+        chosen, gathered, (((0,), (0,)), ((), ())), preferred_element_type=jnp.float32
+    )
+    updated = (residual + expert_out).astype(jnp.bfloat16).reshape(tables, cells, width)
+    updated = jnp.where(mine == 0, updated, updated[::-1])
+    return jnp.transpose(updated, (1, 0, 2))
 
 
 def from_partner(block, axis, bit):
@@ -181,8 +509,9 @@
         P(("expert", "head"), None),
         P(("expert", "head"), None),
     )
+    pairs = mesh.shape["expert"] == 4 and mesh.shape["head"] == 8
     return jax.shard_map(
-        shards,
+        paired_shards if pairs else shards,
         mesh=mesh,
         in_specs=placed,
         out_specs=P(("expert", "head"), None, None),

time: 378 us -> 278 us (0.74)
  waiting for transfers between devices: 190 us -> 116 us
  matrix products: 52.9 us -> 0.35 us
  starting transfers between devices: 3.89 us -> 48.2 us
  Pallas kernels: 0 us -> 41.9 us
  local copies, waits for them, and re-layouts: 62.5 us -> 21.2 us
  other arithmetic: 24 us -> 4.91 us
    all_gather x3 -> x2, waiting for transfers between devices: 112 us -> 32.3 us  [the longest x1 32.3 us: paired_shards(): parts = lax.all_gather(part, 'head', axis=0, tiled=False)]
    dot_general x14 -> x1, matrix products: 52.9 us -> 0.35 us  [paired_shards(): lax.dot_general(chosen, gathered, (((0,), (0,)), ((), ())), preferred_ele...]
    ppermute x2 -> x43, waiting for transfers between devices: 5.18 us -> 55.9 us  [the longest x12 21.4 us: along_z(): return lax.ppermute(block, 'head', route)]
    reduce_scatter x1 -> x0, waiting for transfers between devices: 49.2 us -> none  [shards(): lax.psum_scatter(product.reshape(count_rows, tables, model_width).astype(...]
    ppermute x2 -> x43, starting transfers between devices: 0.21 us -> 45.5 us  [the longest x12 21.1 us: along_z(): return lax.ppermute(block, 'head', route)]
    pallas_call x0 -> x7, Pallas kernels: none -> 41.9 us  [local_call(): pl.pallas_call(body, out_shape=outs, in_specs=specs, out_specs=[VMEM] * l...]
    reshape x7 -> x1, local copies, waits for them, and re-layouts: 30.3 us -> 0.6 us  [paired_shards(): norm_gain.reshape(1, width)]
    reduce_sum x5 -> x0, other arithmetic: 14.4 us -> none  [the longest x4 13 us: step(): running_sum = running_sum * factor + jnp.sum(exp_scores, axis=-1)]
  transfers between devices with their start and end apart: 7 -> 46, of which waited for: 7 -> 18; matrix products, arithmetic and copies ran while one was open for 4% -> 6% of each run, Pallas kernels for 0% -> 9%
where the time goes in v1:
time: 278 us; the launch traced here: 277 us
  waiting for transfers between devices  116 us (42%)
  starting transfers between devices  48.2 us (17%)
  Pallas kernels  41.9 us (15%)
  blocking collectives  30.6 us (11%)
  local copies, waits for them, and re-layouts  21.2 us (8%)
  between operations  14 us (5%)
  other arithmetic  4.91 us (2%)
    pallas_call x7, Pallas kernels, local_call(): pl.pallas_call(body, out_shape=outs, in_specs=specs, out_specs=[VMEM] * l...  41.9 us
    all_gather x1, waiting for transfers between devices, paired_shards(): parts = lax.all_gather(part, 'head', axis=0, tiled=False)  32.3 us
    all_to_all x1, blocking collectives, paired_shards(): lax.all_to_all(send_rows.reshape(2 * expert_count, slot_cap // 2, width),...  30.6 us
    all_to_all x1, waiting for transfers between devices, paired_shards(): lax.all_to_all(merged.reshape(2 * expert_count, slot_cap // 2, width), ev...  27.5 us
    ppermute x12, waiting for transfers between devices, along_z(): return lax.ppermute(block, 'head', route)  21.4 us
    ppermute x12, starting transfers between devices, along_z(): return lax.ppermute(block, 'head', route)  21.1 us
    ppermute x9, waiting for transfers between devices, in_plane(): return lax.ppermute(block, 'expert', [(e, e ^ bits) for e in range(count)])  16.6 us
    unnamed x102, local copies, waits for them, and re-layouts  12.6 us
  transfers between devices with their start and end apart: 46, of which 18 were waited for; matrix products, arithmetic and copies ran while one was open for 6% of the time, Pallas kernels for 9%

profile of v1, /device:TPU:0, one launch (start us, length us, event | category | flops | bytes accessed | tf_op | source)
XLA Modules:
  0.0 277.0 jit_solution(5457216050932108421)
XLA Ops:
  8.6 32.3 %all-gather.5.cloned.1.call-done = bf16[512,2048]{1,0:T(8,128)(2,1)} async-done(((bf16[64,2048]{1,0:T(8,128)(2,1)}), bf16[512,2048]{1,0:T(8,128)(2,1)}) %all-gather.5.cloned.1.call-update) | async-done | bytes 2097168 | tf_op jit(solution)/shard_map/all_gather | solution.py:282
  42.5 5.2 %collective-permute-start.2 = (bf16[64,2048]{1,0:T(8,128)(2,1)S(1)}, bf16[64,2048]{1,0:T(8,128)(2,1)}, u32[]{:S(2)}, u32[]{:S(2)}) collective-permute-start(bf16[64,2048]{1,0:T(8,128)(2,1)S(1)} %get-tuple-element.62.refs_0_), channel_id=1, source_target_pairs={{0,2},{1,3},{2,4},{3,5},{4,6},{5,7},{8,10},{9,11},{10,12},{11,13},... | collective-permute-start | bytes 786440 | tf_op jit(solution)/shard_map/ppermute | solution.py:48
  49.1 5.3 %collective-permute-start.4 = (bf16[64,2048]{1,0:T(8,128)(2,1)S(1)}, bf16[64,2048]{1,0:T(8,128)(2,1)}, u32[]{:S(2)}, u32[]{:S(2)}) collective-permute-start(bf16[64,2048]{1,0:T(8,128)(2,1)S(1)} %get-tuple-element.61.refs_2_), channel_id=1, source_target_pairs={{0,2},{1,3},{2,4},{3,5},{4,6},{5,7},{8,10},{9,11},{10,12},{11,13},... | collective-permute-start | bytes 786440 | tf_op jit(solution)/shard_map/ppermute | solution.py:48
  67.2 6.0 %collective-permute-done.13 = bf16[64,2048]{1,0:T(8,128)(2,1)S(1)} collective-permute-done((bf16[64,2048]{1,0:T(8,128)(2,1)S(1)}, bf16[64,2048]{1,0:T(8,128)(2,1)S(1)}, u32[]{:S(2)}, u32[]{:S(2)}) %collective-permute-start.13) | collective-permute-done | bytes 262176 | tf_op jit(solution)/shard_map/ppermute | solution.py:48
  75.8 7.5 %collective-permute-done.16 = bf16[64,2048]{1,0:T(8,128)(2,1)S(1)} collective-permute-done((bf16[64,2048]{1,0:T(8,128)(2,1)}, bf16[64,2048]{1,0:T(8,128)(2,1)S(1)}, u32[]{:S(2)}, u32[]{:S(2)}) %collective-permute-start.16) | collective-permute-done | bytes 262176 | tf_op jit(solution)/shard_map/ppermute | solution.py:48
  87.3 6.3 %shard_map.118 = (bf16[384,384]{1,0:T(8,128)(2,1)}, bf16[384,384]{1,0:T(8,128)(2,1)}, bf16[384,384]{1,0:T(8,128)(2,1)}, bf16[384,384]{1,0:T(8,128)(2,1)}) custom-call(bf16[64,2048]{1,0:T(8,128)(2,1)} %copy-done.17, bf16[64,2048]{1,0:T(8,128)(2,1)} %collective-permute-done.refs_1_, bf16[64,2048]{1,0:T(8,128)(2,1)} %copy-done.16, bf16[64,2048]{1,0:T(8,128)(2,1)} %copy-done.36, ...), custom_call_target="tpu_custom_call" | custom-call | flops 2415919104 | bytes 7471104 | tf_op jit(solution)/shard_map/pallas_call | solution.py:20
  97.4 7.9 %collective-permute-done.25 = bf16[64,2048]{1,0:T(8,128)(2,1)S(1)} collective-permute-done((bf16[64,2048]{1,0:T(8,128)(2,1)S(1)}, bf16[64,2048]{1,0:T(8,128)(2,1)S(1)}, u32[]{:S(2)}, u32[]{:S(2)}) %collective-permute-start.25) | collective-permute-done | bytes 262176 | tf_op jit(solution)/shard_map/ppermute | solution.py:48
  108.2 3.9 %shard_map.119 = (bf16[128,384]{1,0:T(8,128)(2,1)}, bf16[128,384]{1,0:T(8,128)(2,1)}, bf16[128,384]{1,0:T(8,128)(2,1)}, bf16[128,384]{1,0:T(8,128)(2,1)}) custom-call(bf16[64,2048]{1,0:T(8,128)(2,1)} %copy-done.5, bf16[64,2048]{1,0:T(8,128)(2,1)} %copy-done.12, bf16[64,2048]{1,0:T(8,128)(2,1)} %copy-done.6, bf16[64,2048]{1,0:T(8,128)(2,1)} %copy-done.13, ...), custom_call_target="tpu_custom_call" | custom-call | flops 805306368 | bytes 4587520 | tf_op jit(solution)/shard_map/pallas_call | solution.py:20
  116.4 3.9 %shard_map.120 = (bf16[128,384]{1,0:T(8,128)(2,1)}, bf16[128,384]{1,0:T(8,128)(2,1)}, bf16[128,384]{1,0:T(8,128)(2,1)}, bf16[128,384]{1,0:T(8,128)(2,1)}) custom-call(bf16[64,2048]{1,0:T(8,128)(2,1)} %copy-done.7, bf16[64,2048]{1,0:T(8,128)(2,1)} %copy-done.14, bf16[64,2048]{1,0:T(8,128)(2,1)} %copy-done.8, bf16[64,2048]{1,0:T(8,128)(2,1)} %copy-done.15, ...), custom_call_target="tpu_custom_call" | custom-call | flops 805306368 | bytes 4587520 | tf_op jit(solution)/shard_map/pallas_call | solution.py:20
  121.0 7.0 %collective-permute-done.11.refs_2_ = bf16[384,384]{1,0:T(8,128)(2,1)S(1)} collective-permute-done((bf16[384,384]{1,0:T(8,128)(2,1)}, bf16[384,384]{1,0:T(8,128)(2,1)S(1)}, u32[]{:S(2)}, u32[]{:S(2)}) %collective-permute-start.11) | collective-permute-done | bytes 294944 | tf_op jit(solution)/shard_map/ppermute | solution.py:58
  128.6 2.1 collective-permute-start.29
  131.9 2.4 collective-permute-done.20.refs_6_
  136.0 3.1 %collective-permute-done.29.refs_10_ = bf16[128,384]{1,0:T(8,128)(2,1)S(1)} collective-permute-done((bf16[128,384]{1,0:T(8,128)(2,1)}, bf16[128,384]{1,0:T(8,128)(2,1)S(1)}, u32[]{:S(2)}, u32[]{:S(2)}) %collective-permute-start.29) | collective-permute-done | bytes 98336 | tf_op jit(solution)/shard_map/ppermute | solution.py:58
  139.1 2.3 collective-permute-done.30.refs_11_
  142.1 8.9 %shard_map.121 = (bf16[512,128]{1,0:T(8,128)(2,1)}, bf16[512,128]{1,0:T(8,128)(2,1)}, bf16[512,128]{1,0:T(8,128)(2,1)}, bf16[512,128]{1,0:T(8,128)(2,1)}) custom-call(s32[1]{0:T(128)} %bitcast.place_ref, f32[1,2048]{1,0:T(1,128)} %select_n.131.bias_ref, bf16[384,384]{1,0:T(8,128)(2,1)} %get-tuple-element.33.refs_0_, bf16[384,384]{1,0:T(8,128)(2,1)} %copy-done.32, ...), custom_call_target="tpu_custom_call" | custom-call | flops 2147483648 | bytes 2498564 | tf_op jit(solution)/shard_map/pallas_call | solution.py:20
  157.1 8.6 %collective-permute-done.32.refs_2_ = bf16[512,128]{1,0:T(8,128)(2,1)S(1)} collective-permute-done((bf16[512,128]{1,0:T(8,128)(2,1)}, bf16[512,128]{1,0:T(8,128)(2,1)S(1)}, u32[]{:S(2)}, u32[]{:S(2)}) %collective-permute-start.32) | collective-permute-done | bytes 131104 | tf_op jit(solution)/shard_map/ppermute | solution.py:53
  181.4 6.7 %shard_map.123 = (f32[128,2048]{1,0:T(8,128)}, bf16[256,2048]{1,0:T(8,128)(2,1)}) custom-call(s32[3]{0:T(128)} %pad_add_fusion.place_ref, bf16[128,2048]{1,0:T(8,128)(2,1)} %bitcast.36, s32[128,1]{1,0:T(8,128)} %reshape.320.live_ref, s32[1,128]{1,0:T(1,128)} %select_n.127.target_ref, bf16[1,2048]{1,0:T(2,128)(2,1)} %reshape.293.gain_ref, ...), custom_call_target="tpu_custom_call" | custom-call | flops 1207959552 | bytes 11539468 | tf_op jit(solution)/shard_map/pallas_call | solution.py:20
  188.0 30.6 %all_to_all.10 = bf16[32,8,2048]{2,1,0:T(8,128)(2,1)S(1)} all-to-all(bf16[32,8,2048]{2,1,0:T(8,128)(2,1)} %bitcast.40), channel_id=1, replica_groups=mesh['expert'=4,'head'=8] {'expert','head'}, dimensions={0} | all-to-all | bytes 2097152 | tf_op jit(solution)/shard_map/all_to_all | solution.py:314
  218.6 2.7 collective-permute-done.41.other_ref
  222.3 10.2 %shard_map.124 = (bf16[256,2048]{1,0:T(8,128)(2,1)}, bf16[256,2048]{1,0:T(8,128)(2,1)}) custom-call(bf16[256,2048]{1,0:T(8,128)(2,1)} %bitcast.42, bf16[256,2048]{1,0:T(8,128)(2,1)} %copy-done.31, bf16[704,2048]{1,0:T(8,128)(2,1)} %bitcast.43, bf16[704,2048]{1,0:T(8,128)(2,1)} %bitcast.44, bf16[704,2048]{1,0:T(8,128)(2,1)} %bitcast.45), custom_call_target="tpu_custom_call" | custom-call | flops 4429185024 | bytes 12845056 | tf_op jit(solution)/shard_map/pallas_call | solution.py:20
  232.6 2.7 collective-permute-done.42
  235.4 2.6 fusion
  238.0 2.6 all-to-all-start.1
  240.7 27.5 %all-to-all-done.1 = bf16[32,8,2048]{2,1,0:T(8,128)(2,1)S(1)} async-done(((bf16[32,8,2048]{2,1,0:T(8,128)(2,1)}), bf16[32,8,2048]{2,1,0:T(8,128)(2,1)S(1)}, u32[]{:S(2)}, u32[]{:S(2)}) %all-to-all-start.1) | async-done | bytes 1048608 | tf_op jit(solution)/shard_map/all_to_all | solution.py:327
  (215 shorter events, 64.6 us)
Async XLA Ops:
  6.5 34.3 %all-gather.5.cloned.1.call-start = ((), (), s32[]{:S(2)}) async-start(), calls=%async_computation.2 | async-start | bytes 2359296 | tf_op jit(solution)/shard_map/all_gather | solution.py:282
  8.5 172.2 %all-gather.7.cloned.1.call-start = ((), (), s32[]{:S(2)}) async-start(), calls=%async_computation.3 | async-start | bytes 10485760 | tf_op jit(solution)/shard_map/all_gather | solution.py:283
  41.2 21.3 %collective-permute-start.6 = (bf16[64,2048]{1,0:T(8,128)(2,1)S(1)}, bf16[64,2048]{1,0:T(8,128)(2,1)S(1)}, u32[]{:S(2)}, u32[]{:S(2)}) collective-permute-start(bf16[64,2048]{1,0:T(8,128)(2,1)S(1)} %get-tuple-element.62.refs_0_), channel_id=1, source_target_pairs={{2,0},{3,1},{4,2},{5,3},{6,4},{7,5},{10,8},{11,9},{12,10},{13,11},... | collective-permute-start | bytes 786440 | tf_op jit(solution)/shard_map/ppermute | solution.py:48
  42.5 21.3 %collective-permute-start.2 = (bf16[64,2048]{1,0:T(8,128)(2,1)S(1)}, bf16[64,2048]{1,0:T(8,128)(2,1)}, u32[]{:S(2)}, u32[]{:S(2)}) collective-permute-start(bf16[64,2048]{1,0:T(8,128)(2,1)S(1)} %get-tuple-element.62.refs_0_), channel_id=1, source_target_pairs={{0,2},{1,3},{2,4},{3,5},{4,6},{5,7},{8,10},{9,11},{10,12},{11,13},... | collective-permute-start | bytes 786440 | tf_op jit(solution)/shard_map/ppermute | solution.py:48
  47.8 18.7 %collective-permute-start.8 = (bf16[64,2048]{1,0:T(8,128)(2,1)S(1)}, bf16[64,2048]{1,0:T(8,128)(2,1)}, u32[]{:S(2)}, u32[]{:S(2)}) collective-permute-start(bf16[64,2048]{1,0:T(8,128)(2,1)S(1)} %get-tuple-element.61.refs_2_), channel_id=1, source_target_pairs={{2,0},{3,1},{4,2},{5,3},{6,4},{7,5},{10,8},{11,9},{12,10},{13,11},... | collective-permute-start | bytes 786440 | tf_op jit(solution)/shard_map/ppermute | solution.py:48
  49.1 18.0 %collective-permute-start.4 = (bf16[64,2048]{1,0:T(8,128)(2,1)S(1)}, bf16[64,2048]{1,0:T(8,128)(2,1)}, u32[]{:S(2)}, u32[]{:S(2)}) collective-permute-start(bf16[64,2048]{1,0:T(8,128)(2,1)S(1)} %get-tuple-element.61.refs_2_), channel_id=1, source_target_pairs={{0,2},{1,3},{2,4},{3,5},{4,6},{5,7},{8,10},{9,11},{10,12},{11,13},... | collective-permute-start | bytes 786440 | tf_op jit(solution)/shard_map/ppermute | solution.py:48
  54.3 20.8 %collective-permute-start = (bf16[64,2048]{1,0:T(8,128)(2,1)S(1)}, bf16[64,2048]{1,0:T(8,128)(2,1)}, u32[]{:S(2)}, u32[]{:S(2)}) collective-permute-start(bf16[64,2048]{1,0:T(8,128)(2,1)S(1)} %get-tuple-element.62.refs_0_), channel_id=1, source_target_pairs={{0,1},{1,0},{2,3},{3,2},{4,5},{5,4},{6,7},{7,6},{8,9},{9,8},{10,11... | collective-permute-start | bytes 786440 | tf_op jit(solution)/shard_map/ppermute | solution.py:37
  62.5 10.6 %collective-permute-start.13 = (bf16[64,2048]{1,0:T(8,128)(2,1)S(1)}, bf16[64,2048]{1,0:T(8,128)(2,1)S(1)}, u32[]{:S(2)}, u32[]{:S(2)}) collective-permute-start(bf16[64,2048]{1,0:T(8,128)(2,1)S(1)} %collective-permute-done.6.refs_8_), channel_id=1, source_target_pairs={{2,0},{3,1},{4,2},{5,3},{10,8},{11,9},{12,10},{13,11},{18,16},{19,... | collective-permute-start | bytes 786440 | tf_op jit(solution)/shard_map/ppermute | solution.py:48
  67.1 17.5 %collective-permute-start.3 = (bf16[64,2048]{1,0:T(8,128)(2,1)}, bf16[64,2048]{1,0:T(8,128)(2,1)S(1)}, u32[]{:S(2)}, u32[]{:S(2)}) collective-permute-start(bf16[64,2048]{1,0:T(8,128)(2,1)} %collective-permute-done.2.refs_4_), channel_id=1, source_target_pairs={{0,1},{1,0},{2,3},{3,2},{4,5},{5,4},{6,7},{7,6},{8,9},{9,8},{10,11... | collective-permute-start | bytes 786440 | tf_op jit(solution)/shard_map/ppermute | solution.py:37
  75.3 10.6 %collective-permute-start.7 = (bf16[64,2048]{1,0:T(8,128)(2,1)S(1)}, bf16[64,2048]{1,0:T(8,128)(2,1)S(1)}, u32[]{:S(2)}, u32[]{:S(2)}) collective-permute-start(bf16[64,2048]{1,0:T(8,128)(2,1)S(1)} %collective-permute-done.6.refs_8_), channel_id=1, source_target_pairs={{0,1},{1,0},{2,3},{3,2},{4,5},{5,4},{6,7},{7,6},{8,9},{9,8},{10,11... | collective-permute-start | bytes 786440 | tf_op jit(solution)/shard_map/ppermute | solution.py:37
  83.3 11.9 %collective-permute-start.22 = (bf16[64,2048]{1,0:T(8,128)(2,1)S(1)}, bf16[64,2048]{1,0:T(8,128)(2,1)S(1)}, u32[]{:S(2)}, u32[]{:S(2)}) collective-permute-start(bf16[64,2048]{1,0:T(8,128)(2,1)S(1)} %collective-permute-done.13), channel_id=1, source_target_pairs={{2,0},{3,1},{10,8},{11,9},{18,16},{19,17},{26,24},{27,25}} | collective-permute-start | bytes 786440 | tf_op jit(solution)/shard_map/ppermute | solution.py:48
  84.6 11.9 %collective-permute-start.23 = (bf16[64,2048]{1,0:T(8,128)(2,1)S(1)}, bf16[64,2048]{1,0:T(8,128)(2,1)S(1)}, u32[]{:S(2)}, u32[]{:S(2)}) collective-permute-start(bf16[64,2048]{1,0:T(8,128)(2,1)S(1)} %collective-permute-done.14), channel_id=1, source_target_pairs={{4,6},{5,7},{12,14},{13,15},{20,22},{21,23},{28,30},{29,31}} | collective-permute-start | bytes 786440 | tf_op jit(solution)/shard_map/ppermute | solution.py:48
  85.3 21.5 %collective-permute-start.15 = (bf16[64,2048]{1,0:T(8,128)(2,1)S(1)}, bf16[64,2048]{1,0:T(8,128)(2,1)S(1)}, u32[]{:S(2)}, u32[]{:S(2)}) collective-permute-start(bf16[64,2048]{1,0:T(8,128)(2,1)S(1)} %broadcast_select_fusion.3.refs_0_), channel_id=1, source_target_pairs={{0,1},{1,0},{2,3},{3,2},{4,5},{5,4},{6,7},{7,6},{8,9},{9,8},{10,11... | collective-permute-start | bytes 786440 | tf_op jit(solution)/shard_map/ppermute | solution.py:37
  85.9 21.5 %collective-permute-start.18 = (bf16[64,2048]{1,0:T(8,128)(2,1)S(1)}, bf16[64,2048]{1,0:T(8,128)(2,1)S(1)}, u32[]{:S(2)}, u32[]{:S(2)}) collective-permute-start(bf16[64,2048]{1,0:T(8,128)(2,1)S(1)} %broadcast_select_fusion.2.refs_2_), channel_id=1, source_target_pairs={{0,1},{1,0},{2,3},{3,2},{4,5},{5,4},{6,7},{7,6},{8,9},{9,8},{10,11... | collective-permute-start | bytes 786440 | tf_op jit(solution)/shard_map/ppermute | solution.py:37
  93.7 26.7 %collective-permute-start.10 = (bf16[384,384]{1,0:T(8,128)(2,1)}, bf16[384,384]{1,0:T(8,128)(2,1)S(1)}, u32[]{:S(2)}, u32[]{:S(2)}) collective-permute-start(bf16[384,384]{1,0:T(8,128)(2,1)} %get-tuple-element.34), channel_id=1, source_target_pairs={{0,8},{8,0},{16,24},{24,16},{1,9},{9,1},{17,25},{25,17},{2,10},{10... | collective-permute-start | bytes 884744 | tf_op jit(solution)/shard_map/ppermute | solution.py:58
  105.3 22.7 %collective-permute-start.11 = (bf16[384,384]{1,0:T(8,128)(2,1)}, bf16[384,384]{1,0:T(8,128)(2,1)S(1)}, u32[]{:S(2)}, u32[]{:S(2)}) collective-permute-start(bf16[384,384]{1,0:T(8,128)(2,1)} %get-tuple-element.35), channel_id=1, source_target_pairs={{0,16},{8,24},{16,0},{24,8},{1,17},{9,25},{17,1},{25,9},{2,18},{10... | collective-permute-start | bytes 884744 | tf_op jit(solution)/shard_map/ppermute | solution.py:58
  106.9 21.7 %collective-permute-start.12 = (bf16[384,384]{1,0:T(8,128)(2,1)}, bf16[384,384]{1,0:T(8,128)(2,1)S(1)}, u32[]{:S(2)}, u32[]{:S(2)}) collective-permute-start(bf16[384,384]{1,0:T(8,128)(2,1)} %get-tuple-element.36), channel_id=1, source_target_pairs={{0,24},{8,16},{16,8},{24,0},{1,25},{9,17},{17,9},{25,1},{2,26},{10... | collective-permute-start | bytes 884744 | tf_op jit(solution)/shard_map/ppermute | solution.py:58
  112.1 18.6 %collective-permute-start.19 = (bf16[128,384]{1,0:T(8,128)(2,1)}, bf16[128,384]{1,0:T(8,128)(2,1)S(1)}, u32[]{:S(2)}, u32[]{:S(2)}) collective-permute-start(bf16[128,384]{1,0:T(8,128)(2,1)} %get-tuple-element.38), channel_id=1, source_target_pairs={{0,8},{8,0},{16,24},{24,16},{1,9},{9,1},{17,25},{25,17},{2,10},{10... | collective-permute-start | bytes 294920 | tf_op jit(solution)/shard_map/ppermute | solution.py:58
  114.9 19.4 %collective-permute-start.20 = (bf16[128,384]{1,0:T(8,128)(2,1)}, bf16[128,384]{1,0:T(8,128)(2,1)S(1)}, u32[]{:S(2)}, u32[]{:S(2)}) collective-permute-start(bf16[128,384]{1,0:T(8,128)(2,1)} %get-tuple-element.39), channel_id=1, source_target_pairs={{0,16},{8,24},{16,0},{24,8},{1,17},{9,25},{17,1},{25,9},{2,18},{10... | collective-permute-start | bytes 294920 | tf_op jit(solution)/shard_map/ppermute | solution.py:58
  120.4 14.0 %collective-permute-start.21 = (bf16[128,384]{1,0:T(8,128)(2,1)S(1)}, bf16[128,384]{1,0:T(8,128)(2,1)S(1)}, u32[]{:S(2)}, u32[]{:S(2)}) collective-permute-start(bf16[128,384]{1,0:T(8,128)(2,1)S(1)} %copy-done.43), channel_id=1, source_target_pairs={{0,24},{8,16},{16,8},{24,0},{1,25},{9,17},{17,9},{25,1},{2,26},{10... | collective-permute-start | bytes 294920 | tf_op jit(solution)/shard_map/ppermute | solution.py:58
  130.7 10.8 %collective-permute-start.30 = (bf16[128,384]{1,0:T(8,128)(2,1)}, bf16[128,384]{1,0:T(8,128)(2,1)S(1)}, u32[]{:S(2)}, u32[]{:S(2)}) collective-permute-start(bf16[128,384]{1,0:T(8,128)(2,1)} %get-tuple-element.44), channel_id=1, source_target_pairs={{0,24},{8,16},{16,8},{24,0},{1,25},{9,17},{17,9},{25,1},{2,26},{10... | collective-permute-start | bytes 294920 | tf_op jit(solution)/shard_map/ppermute | solution.py:58
  152.8 12.9 %collective-permute-start.32 = (bf16[512,128]{1,0:T(8,128)(2,1)}, bf16[512,128]{1,0:T(8,128)(2,1)S(1)}, u32[]{:S(2)}, u32[]{:S(2)}) collective-permute-start(bf16[512,128]{1,0:T(8,128)(2,1)} %get-tuple-element.47), channel_id=1, source_target_pairs={{0,4},{1,5},{2,6},{3,7},{4,0},{5,1},{6,2},{7,3},{8,12},{9,13},{10,... | collective-permute-start | bytes 393224 | tf_op jit(solution)/shard_map/ppermute | solution.py:53
  153.9 11.8 %collective-permute-start.33 = (bf16[512,128]{1,0:T(8,128)(2,1)}, bf16[512,128]{1,0:T(8,128)(2,1)S(1)}, u32[]{:S(2)}, u32[]{:S(2)}) collective-permute-start(bf16[512,128]{1,0:T(8,128)(2,1)} %get-tuple-element.48), channel_id=1, source_target_pairs={{0,2},{1,3},{2,4},{3,5},{4,6},{5,7},{6,0},{7,1},{8,10},{9,11},{10,... | collective-permute-start | bytes 393224 | tf_op jit(solution)/shard_map/ppermute | solution.py:53
  238.0 30.2 %all-to-all-start.1 = ((bf16[32,8,2048]{2,1,0:T(8,128)(2,1)}), bf16[32,8,2048]{2,1,0:T(8,128)(2,1)S(1)}, u32[]{:S(2)}, u32[]{:S(2)}) async-start(bf16[32,8,2048]{2,1,0:T(8,128)(2,1)} %fusion), calls=%async_computation.1 | async-start | bytes 2097152 | tf_op jit(solution)/shard_map/all_to_all | solution.py:327
  (70 other events, 700.4 us)
Sparse Core Ops, SparseCore 0:
  9.0 31.7 all-gather.4
  42.7 108.1 all-gather.6

commit v2 on v0

--- a/solution.py
+++ b/solution.py
@@ -1,11 +1,408 @@
+import functools
 import math
 
 import jax
 import jax.numpy as jnp
 from jax import lax
+from jax.experimental import pallas as pl
+from jax.experimental.pallas import tpu as pltpu
 from jax.sharding import PartitionSpec as P
 
 DH = 128
+VMEM = pl.BlockSpec(memory_space=pltpu.VMEM)
+SMEM = pl.BlockSpec(memory_space=pltpu.SMEM)
+ROWS_BY_ROWS = (((1,), (1,)), ((), ()))
+
+
+def local_call(body, outs, args, specs, flops, scratch=(), grant=60):
+    moved = sum(a.size * a.dtype.itemsize for a in list(args) + list(outs))
+    return pl.pallas_call(
+        body,
+        out_shape=outs,
+        in_specs=specs,
+        out_specs=[VMEM] * len(outs),
+        scratch_shapes=list(scratch),
+        compiler_params=pltpu.CompilerParams(vmem_limit_bytes=grant * 1024 * 1024),
+        cost_estimate=pl.CostEstimate(flops=flops, bytes_accessed=moved, transcendentals=0),
+    )(*args)
+
+
+def shape_of(dims, dtype=jnp.bfloat16):
+    return jax.ShapeDtypeStruct(dims, dtype)
+
+
+def swap_cores(block):
+    count = lax.axis_size("head")
+    return lax.ppermute(block, "head", [(h, h ^ 1) for h in range(count)])
+
+
+def neighbours(block, first):
+    planes = lax.axis_size("head") // 2
+    route = []
+    for low in range(first, planes - 1, 2):
+        for core in range(2):
+            here, there = 2 * low + core, 2 * low + 2 + core
+            route += [(here, there), (there, here)]
+    return lax.ppermute(block, "head", route)
+
+
+def outwards(block):
+    route = [(2 * a + core, 2 * b + core) for a, b in ((1, 0), (2, 3)) for core in range(2)]
+    return lax.ppermute(block, "head", route)
+
+
+def across_z(block, bits):
+    count = lax.axis_size("head")
+    return lax.ppermute(block, "head", [(h, h ^ (2 * bits)) for h in range(count)])
+
+
+def in_plane(block, bits):
+    count = lax.axis_size("expert")
+    return lax.ppermute(block, "expert", [(e, e ^ bits) for e in range(count)])
+
+
+def stack_body(*refs):
+    half = refs[0].shape[0] // 2
+    for index, ref in enumerate(refs[:-2]):
+        for side in range(2):
+            refs[side - 2][pl.ds(index * half, half), :] = ref[pl.ds(side * half, half), :]
+
+
+def stack(blocks):
+    rows, width = blocks[0].shape
+    shape = shape_of((len(blocks) * rows // 2, width))
+    return local_call(stack_body, [shape] * 2, blocks, [VMEM] * len(blocks), 0)
+
+
+def choose_body(place_ref, *refs):
+    out_ref = refs[-1]
+    for side in range(2):
+        start = pl.multiple_of((place_ref[0] ^ side) * DH, DH)
+        for index, ref in enumerate(refs[:-1]):
+            out_ref[:, pl.ds((3 * side + index) * DH, DH)] = ref[:, pl.ds(start, DH)]
+
+
+def project_body(pieces, half, *refs):
+    inputs, weight_ref, outs = refs[: 2 * pieces], refs[2 * pieces], refs[2 * pieces + 1 :]
+    width = weight_ref.shape[1] // 2
+    rows = []
+    for table in range(2):
+        for piece in range(pieces):
+            for side in range(2):
+                rows.append(inputs[2 * piece + side][pl.ds(table * half, half), :])
+    mixed = jnp.dot(
+        jnp.concatenate(rows, axis=0), weight_ref[...], preferred_element_type=jnp.float32
+    ).astype(jnp.bfloat16)
+    count = pieces * 2 * half
+    for table in range(2):
+        for side in range(2):
+            outs[2 * table + side][...] = mixed[
+                table * count : (table + 1) * count, side * width : (side + 1) * width
+            ]
+
+
+def project(blocks, weight):
+    pieces, half, width = len(blocks), blocks[0][0].shape[0] // 2, weight.shape[1] // 2
+    args = [block for pair in blocks for block in pair] + [weight]
+    return local_call(
+        functools.partial(project_body, pieces, half),
+        [shape_of((pieces * 2 * half, width))] * 4,
+        args,
+        [VMEM] * len(args),
+        2 * pieces * 4 * half * weight.size,
+        grant=20,
+    )
+
+
+def attend_body(block, place_ref, bias_ref, *refs):
+    early, middle, late = refs[:4], refs[4:8], refs[8:12]
+    out_ref, (keys, values) = refs[12], refs[13:]
+    spot, place, core = place_ref[0], place_ref[1], place_ref[2]
+    planes = 4
+    half = block // 2
+    for source in range(4):
+        parts = (
+            early[source][pl.ds(0, block), :],
+            early[source][pl.ds(block, block), :],
+            middle[source][...],
+            late[source][...],
+        )
+        for slot in range(planes):
+            span = pl.ds((slot * 4 + source) * block, block)
+            keys[span, :] = parts[slot][:, DH : 2 * DH]
+            values[span, :] = parts[slot][:, 2 * DH :]
+    scale = 1.0 / math.sqrt(DH) * math.log2(math.e)
+    third = jnp.where(place < 2, 2, 1)
+    fourth = jnp.where(place < 2, 3, 0)
+
+    def queries(slot, source):
+        if slot < 2:
+            return early[source][pl.ds(slot * block, block), pl.ds(0, DH)]
+        return (middle, late)[slot - 2][source][:, pl.ds(0, DH)]
+
+    for slot, plane in enumerate((place, place ^ 1, third, fourth)):
+        for first in (0, 2):
+            rows = jnp.concatenate([queries(slot, first), queries(slot, first + 1)], axis=0)
+            scores = lax.dot_general(
+                rows, keys[...], ROWS_BY_ROWS, preferred_element_type=jnp.float32
+            )
+            scores = scores + bias_ref[...]
+            top = jnp.max(scores, axis=1, keepdims=True)
+            weights = jnp.exp2((scores - top) * scale)
+            total = jnp.sum(weights, axis=1, keepdims=True)
+            mixed = jnp.dot(
+                weights.astype(jnp.bfloat16), values[...], preferred_element_type=jnp.float32
+            )
+            mixed = (mixed / total).astype(jnp.bfloat16)
+            for index in range(4):
+                source, side = first + index // 2, index % 2
+                device = (spot ^ source) * 2 * planes + 2 * plane + (core ^ side)
+                start = pl.multiple_of(device * half, half)
+                out_ref[pl.ds(start, half), :] = mixed[index * half : (index + 1) * half]
+
+
+def join_body(planes, place_ref, own_ref, live_ref, target_ref, gain_ref, heads_ref, *refs):
+    weights = (refs[:9], refs[9:18])
+    residual_ref, send_ref, joined = refs[18:]
+    spot, place, core = place_ref[0], place_ref[1], place_ref[2]
+    mine = spot // 2
+    block, quarter = joined.shape[0] // 2, weights[0][1].shape[1]
+    pair = 2 * DH
+    for source in range(4):
+        rows = pl.ds(pl.multiple_of((source // 2 ^ mine) * block, block), block)
+        for head in range(2 * planes):
+            columns = pl.ds(head * pair + source % 2 * DH, DH)
+            joined[rows, columns] = heads_ref[
+                pl.ds((source * 2 * planes + head) * block, block), :
+            ]
+    joined[...] = jnp.where(live_ref[...] > 0, joined[...].astype(jnp.float32), 0.0).astype(
+        jnp.bfloat16
+    )
+    squares = jnp.zeros((2 * block, 1), jnp.float32)
+    for bits in range(4):
+        columns = pl.ds(pl.multiple_of((spot ^ bits) * quarter, quarter), quarter)
+        total = own_ref[:, columns].astype(jnp.float32)
+        for side in range(2):
+            for offset in range(planes):
+                device = 2 * (place ^ offset) + (core ^ side)
+                start = pl.multiple_of(device * pair, pair)
+                if offset == 0:
+                    total += jnp.dot(
+                        joined[:, pl.ds(start, pair)],
+                        weights[side][0][:, columns],
+                        preferred_element_type=jnp.float32,
+                    )
+                    continue
+                for half in range(2):
+                    total += jnp.dot(
+                        joined[:, pl.ds(start + half * DH, DH)],
+                        weights[side][1 + 2 * bits + half][pl.ds((offset - 1) * DH, DH), :],
+                        preferred_element_type=jnp.float32,
+                    )
+        residual_ref[:, columns] = total
+        squares += jnp.sum(total * total, axis=1, keepdims=True)
+    residual = residual_ref[...]
+    mean_square = squares / residual.shape[1]
+    normed = residual * lax.rsqrt(mean_square + 1e-06) * gain_ref[...].astype(jnp.float32)
+    slots = send_ref.shape[0]
+    chosen = lax.broadcasted_iota(jnp.int32, (slots, 2 * block), 0) == target_ref[...]
+    send_ref[...] = jnp.dot(
+        chosen.astype(jnp.float32).astype(jnp.bfloat16),
+        normed.astype(jnp.bfloat16),
+        preferred_element_type=jnp.float32,
+    ).astype(jnp.bfloat16)
+
+
+def expert_body(rows_ref, *refs):
+    sources, out_ref, held, arrivals = refs[:6], refs[6], refs[7:13], refs[13]
+    copies = [
+        pltpu.make_async_copy(source, place, arrivals.at[index])
+        for index, (source, place) in enumerate(zip(sources, held))
+    ]
+    for copy in copies:
+        copy.start()
+    rows = rows_ref[...]
+    total = jnp.zeros(rows.shape, jnp.float32)
+    for half in range(2):
+        gate_ref, up_ref, down_ref = held[3 * half : 3 * half + 3]
+        copies[3 * half].wait()
+        gate = lax.dot_general(
+            rows, gate_ref[...], ROWS_BY_ROWS, preferred_element_type=jnp.float32
+        )
+        copies[3 * half + 1].wait()
+        up = lax.dot_general(rows, up_ref[...], ROWS_BY_ROWS, preferred_element_type=jnp.float32)
+        hidden = (gate / (1.0 + jnp.exp(-gate)) * up).astype(jnp.bfloat16)
+        copies[3 * half + 2].wait()
+        total += jnp.dot(hidden, down_ref[...], preferred_element_type=jnp.float32)
+    out_ref[...] = total.astype(jnp.bfloat16)
+
+
+def finish_body(residual_ref, target_ref, blocks_ref, out_ref):
+    slots = blocks_ref.shape[0]
+    rows = residual_ref.shape[0]
+    chosen = target_ref[...] == lax.broadcasted_iota(jnp.int32, (rows, slots), 1)
+    expert_out = jnp.dot(
+        chosen.astype(jnp.float32).astype(jnp.bfloat16),
+        blocks_ref[...],
+        preferred_element_type=jnp.float32,
+    )
+    out_ref[...] = (residual_ref[...] + expert_out).astype(jnp.bfloat16)
+
+
+def paired_shards(
+    table_cells,
+    w_query,
+    w_key,
+    w_value,
+    w_out,
+    norm_gain,
+    w_gate,
+    w_up,
+    w_down,
+    lengths,
+    expert_of_cell,
+    slot_of_cell,
+):
+    cells, tables, width = table_cells.shape
+    heads = lax.axis_size("head")
+    planes = heads // 2
+    spot, place_head = lax.axis_index("expert"), lax.axis_index("head")
+    mine, parity = spot // 2, spot % 2
+    place, core = place_head // 2, place_head % 2
+
+    rows_dev = cells * tables
+    first, second = table_cells[:, 0], table_cells[:, 1]
+    own = jnp.where(
+        mine == 0,
+        jnp.concatenate([first, second], axis=0),
+        jnp.concatenate([second, first], axis=0),
+    )
+
+    weight = pl.pallas_call(
+        choose_body,
+        out_shape=pltpu.VMEM((width, 6 * DH), w_query.dtype),
+        in_specs=[SMEM] + [VMEM] * 3,
+        out_specs=VMEM,
+        compiler_params=pltpu.CompilerParams(vmem_limit_bytes=56 * 1024 * 1024),
+    )(parity.reshape(1).astype(jnp.int32), w_query, w_key, w_value)
+
+    def spread(outs):
+        return [outs[0]] + [in_plane(outs[bits], bits) for bits in range(1, 4)]
+
+    block = 2 * cells
+    low = place < 2
+    held = jnp.stack([place, place ^ 1, jnp.where(low, 2, 1), jnp.where(low, 3, 0)])
+    sources = jnp.arange(4, dtype=jnp.int32)[None, :, None, None]
+    sides = jnp.arange(2, dtype=jnp.int32)[None, None, :, None]
+    cell = jnp.arange(cells, dtype=jnp.int32)[None, None, None, :]
+    device = (spot ^ sources) * heads + 2 * held[:, None, None, None] + (core ^ sides)
+    count = planes * 4 * block
+    positions = (device * cells + cell).reshape(1, count)
+    bias = jnp.where(positions < lengths[mine], 0.0, -jnp.inf).astype(jnp.float32)
+    where = jnp.stack([spot, place, core]).astype(jnp.int32)
+    own_positions = (spot * heads + place_head) * cells + jnp.arange(cells, dtype=jnp.int32)
+    table_order = jnp.stack([mine, 1 - mine])
+    live = (own_positions[None, :] < lengths[table_order][:, None]).astype(jnp.int32)
+    expert_count = lax.axis_size("expert") * heads // 2
+    slot_cap = 2 * max(1, rows_dev // expert_count)
+    target = (expert_of_cell * slot_cap + slot_of_cell).T
+    target = jnp.where(mine == 0, target, target[::-1]).reshape(1, rows_dev)
+    slots = expert_count * slot_cap
+    live, target, target_column = live.reshape(rows_dev, 1), target, target.reshape(rows_dev, 1)
+    gain = norm_gain.reshape(1, width)
+
+    inside = (place == 1) | (place == 2)
+    beside = neighbours(own, 0)
+    inner = neighbours(own, 1)
+    beside_too = swap_cores(beside)
+    outer = outwards(inner)
+    inner_far = neighbours(beside, 1)
+    quarter = width // 4
+    part = lax.dynamic_slice_in_dim(w_out, spot * quarter, quarter, 1)
+    parts = [across_z(part, bits) for bits in range(1, planes)]
+    small = (bias, where, live, target, target_column, gain)
+    halves = [w_gate[0], w_up[0], w_down[0]]
+    others = [swap_cores(w) for w in halves]
+    inner_far, small, weight, others[0] = lax.optimization_barrier(
+        (inner_far, small, weight, others[0])
+    )
+    bias, where, live, target, target_column, gain = small
+    early_out = project([(own, swap_cores(own)), (beside, beside_too)], weight)
+    early = spread(early_out)
+    outer_far = outwards(inner_far)
+    third = jnp.where(inside, inner, outer)
+    middle_out = project([(third, swap_cores(third))], weight)
+    outer_far, middle_out, early, parts[0], parts[1], others[1] = lax.optimization_barrier(
+        (outer_far, middle_out, early, parts[0], parts[1], others[1])
+    )
+    middle = spread(middle_out)
+    fourth = jnp.where(inside, inner_far, outer_far)
+    late_out = project([(fourth, swap_cores(fourth))], weight)
+    late_out, middle = lax.optimization_barrier((late_out, middle))
+    late = spread(late_out)
+
+    parts, late, others[2] = lax.optimization_barrier((parts, late, others[2]))
+    expert_weights = halves + others
+    far = stack(parts)
+    far, late = lax.optimization_barrier((far, late))
+    shared = early + middle + late
+    fars = [[in_plane(half, bits) for half in far] for bits in (1, 2)]
+    everyone = ("expert", "head")
+    attended = local_call(
+        functools.partial(attend_body, block),
+        [shape_of((count, DH))],
+        [where, bias] + shared,
+        [SMEM] + [VMEM] * 13,
+        4 * count * count * DH,
+        [pltpu.VMEM((count, DH), jnp.bfloat16)] * 2,
+        grant=60,
+    )[0]
+    fars, _ = lax.optimization_barrier((fars, attended))
+    across = [in_plane(fars[1][0], 1), in_plane(fars[0][1], 2)]
+    same = [w_out, *far, *fars[0], *fars[1], *across]
+    out_weights = same + [swap_cores(w) for w in same]
+    arrived = lax.all_to_all(attended, everyone, 0, 0, tiled=True)
+
+    residual, send_rows = local_call(
+        functools.partial(join_body, planes),
+        [shape_of((rows_dev, width), jnp.float32), shape_of((slots, width))],
+        [
+            where,
+            own,
+            live,
+            target,
+            gain,
+            arrived,
+        ]
+        + out_weights,
+        [SMEM] + [VMEM] * 23,
+        2 * rows_dev * width * (width + slots),
+        [pltpu.VMEM((rows_dev, width), jnp.bfloat16)],
+    )
+
+    received = lax.all_to_all(send_rows, everyone, 0, 0, tiled=True)
+    computed = local_call(
+        expert_body,
+        [shape_of((slots, width))],
+        [received] + expert_weights,
+        [VMEM] + [pl.BlockSpec(memory_space=pl.ANY)] * 6,
+        2 * slots * 6 * w_gate.size,
+        [pltpu.VMEM(w.shape, w.dtype) for w in expert_weights] + [pltpu.SemaphoreType.DMA((6,))],
+        grant=60,
+    )[0]
+    gathered = lax.all_to_all(computed, everyone, 0, 0, tiled=True)
+    updated = local_call(
+        finish_body,
+        [shape_of((rows_dev, width))],
+        [residual, target_column, gathered],
+        [VMEM] * 3,
+        2 * rows_dev * width * slots,
+        grant=60,
+    )[0]
+    first, second = updated[:cells], updated[cells:]
+    return jnp.stack(
+        [jnp.where(mine == 0, first, second), jnp.where(mine == 0, second, first)], axis=1
+    )
 
 
 def from_partner(block, axis, bit):
@@ -181,8 +578,9 @@
         P(("expert", "head"), None),
         P(("expert", "head"), None),
     )
+    pairs = mesh.shape["expert"] == 4 and mesh.shape["head"] == 8
     return jax.shard_map(
-        shards,
+        paired_shards if pairs else shards,
         mesh=mesh,
         in_specs=placed,
         out_specs=P(("expert", "head"), None, None),

time: 378 us -> 220 us (0.58)
  waiting for transfers between devices: 190 us -> 85.4 us
  matrix products: 52.9 us -> 0 us
  local copies, waits for them, and re-layouts: 62.5 us -> 13.3 us
  starting transfers between devices: 3.89 us -> 45.8 us
  Pallas kernels: 0 us -> 38.8 us
  other arithmetic: 24 us -> 2.98 us
  between operations: 13.3 us -> 0.46 us
    all_gather x3 -> x0, waiting for transfers between devices: 112 us -> none  [the longest x1 51.5 us: shards(): shard_rows = lax.all_gather(table_cells, 'head', axis=0, tiled=True)]
    ppermute x2 -> x39, waiting for transfers between devices: 5.18 us -> 58.6 us  [the longest x15 28.6 us: in_plane(): return lax.ppermute(block, 'expert', [(e, e ^ bits) for e in range(count)])]
    dot_general x14 -> x0, matrix products: 52.9 us -> none  [the longest x4 16 us: step(): jnp.einsum('shqk,kshd->shqd', exp_scores.astype(jnp.bfloat16), value_bloc...]
    reduce_scatter x1 -> x0, waiting for transfers between devices: 49.2 us -> none  [shards(): lax.psum_scatter(product.reshape(count_rows, tables, model_width).astype(...]
    ppermute x2 -> x39, starting transfers between devices: 0.21 us -> 39.5 us  [the longest x15 18.5 us: in_plane(): return lax.ppermute(block, 'expert', [(e, e ^ bits) for e in range(count)])]
    pallas_call x0 -> x9, Pallas kernels: none -> 38.8 us  [the longest x8 36.3 us: local_call(): pl.pallas_call(body, out_shape=outs, in_specs=specs, out_specs=[VMEM] * l...]
    reshape x7 -> x2, local copies, waits for them, and re-layouts: 30.3 us -> 1.24 us  [the longest x1 0.64 us: paired_shards(): target = jnp.where(mine == 0, target, target[::-1]).reshape(1, rows_dev)]
    reduce_sum x5 -> x0, other arithmetic: 14.4 us -> none  [the longest x4 13 us: step(): running_sum = running_sum * factor + jnp.sum(exp_scores, axis=-1)]
  transfers between devices with their start and end apart: 7 -> 41, of which waited for: 7 -> 19; matrix products, arithmetic and copies ran while one was open for 4% -> 5% of each run, Pallas kernels for 0% -> 8%
where the time goes in v2:
time: 220 us
  waiting for transfers between devices  85.4 us (39%)
  starting transfers between devices  45.8 us (21%)
  Pallas kernels  38.8 us (18%)
  blocking collectives  32.8 us (15%)
  local copies, waits for them, and re-layouts  13.3 us (6%)
  other arithmetic  2.98 us (1%)
    pallas_call x8, Pallas kernels, local_call(): pl.pallas_call(body, out_shape=outs, in_specs=specs, out_specs=[VMEM] * l...  36.3 us
    all_to_all x1, blocking collectives, paired_shards(): received = lax.all_to_all(send_rows, everyone, 0, 0, tiled=True)  32.8 us
    ppermute x15, waiting for transfers between devices, in_plane(): return lax.ppermute(block, 'expert', [(e, e ^ bits) for e in range(count)])  28.6 us
    all_to_all x1, waiting for transfers between devices, paired_shards(): gathered = lax.all_to_all(computed, everyone, 0, 0, tiled=True)  26.8 us
    ppermute x15, starting transfers between devices, in_plane(): return lax.ppermute(block, 'expert', [(e, e ^ bits) for e in range(count)])  18.5 us
    ppermute x3, waiting for transfers between devices, across_z(): lax.ppermute(block, 'head', [(h, h ^ 2 * bits) for h in range(count)])  13 us
    ppermute x2, waiting for transfers between devices, outwards(): return lax.ppermute(block, 'head', route)  11.1 us
    ppermute x3, starting transfers between devices, across_z(): lax.ppermute(block, 'head', [(h, h ^ 2 * bits) for h in range(count)])  10 us
  transfers between devices with their start and end apart: 41, of which 19 were waited for; matrix products, arithmetic and copies ran while one was open for 5% of the time, Pallas kernels for 8%

profile of v2, /device:TPU:0, one launch (start us, length us, event | category | flops | bytes accessed | tf_op | source)
XLA Modules:
  0.0 219.5 jit_solution(7471006083536591659)
XLA Ops:
  0.5 2.1 fusion.1
  3.1 2.7 %collective-permute-start = (bf16[128,2048]{1,0:T(8,128)(2,1)S(1)}, bf16[128,2048]{1,0:T(8,128)(2,1)S(1)}, u32[]{:S(2)}, u32[]{:S(2)}) collective-permute-start(bf16[128,2048]{1,0:T(8,128)(2,1)S(1)} %maximum_select_fusion.refs_0_.own_ref), channel_id=1, source_target_pairs={{0,2},{2,0},{1,3},{3,1},{4,6},{6,4},{5,7},{7,5},{8,10},{10,8},{9,1... | collective-permute-start | bytes 1572872 | tf_op jit(solution)/shard_map/ppermute | solution.py:46
  6.5 1.7 constant_dynamic-slice_fusion
  8.1 4.4 %collective-permute-start.12 = (bf16[256,512]{1,0:T(8,128)(2,1)}, bf16[256,512]{1,0:T(8,128)(2,1)S(1)}, u32[]{:S(2)}, u32[]{:S(2)}) collective-permute-start(bf16[256,512]{1,0:T(8,128)(2,1)} %constant_dynamic-slice_fusion), channel_id=1, source_target_pairs={{0,2},{1,3},{2,0},{3,1},{4,6},{5,7},{6,4},{7,5},{8,10},{9,11},{10,... | collective-permute-start | bytes 786440 | tf_op jit(solution)/shard_map/ppermute | solution.py:56
  14.1 4.5 %collective-permute-done.refs_2_ = bf16[128,2048]{1,0:T(8,128)(2,1)S(1)} collective-permute-done((bf16[128,2048]{1,0:T(8,128)(2,1)S(1)}, bf16[128,2048]{1,0:T(8,128)(2,1)S(1)}, u32[]{:S(2)}, u32[]{:S(2)}) %collective-permute-start) | collective-permute-done | bytes 524320 | tf_op jit(solution)/shard_map/ppermute | solution.py:46
  20.6 3.4 %collective-permute-done.12.refs_0_ = bf16[256,512]{1,0:T(8,128)(2,1)S(1)} collective-permute-done((bf16[256,512]{1,0:T(8,128)(2,1)}, bf16[256,512]{1,0:T(8,128)(2,1)S(1)}, u32[]{:S(2)}, u32[]{:S(2)}) %collective-permute-start.12) | collective-permute-done | bytes 262176 | tf_op jit(solution)/shard_map/ppermute | solution.py:56
  25.2 11.1 %collective-permute-done.5 = bf16[128,2048]{1,0:T(8,128)(2,1)S(1)} collective-permute-done((bf16[128,2048]{1,0:T(8,128)(2,1)S(1)}, bf16[128,2048]{1,0:T(8,128)(2,1)S(1)}, u32[]{:S(2)}, u32[]{:S(2)}) %collective-permute-start.5) | collective-permute-done | bytes 524320 | tf_op jit(solution)/shard_map/ppermute | solution.py:51
  39.1 2.5 %shard_map.118.refs_2_.refs_4_ = bf16[2048,768]{1,0:T(8,128)(2,1)S(1)} custom-call(s32[1]{0:T(128)} %bitcast.13.place_ref, bf16[2048,256]{1,0:T(8,128)(2,1)} %refs_0_.2, bf16[2048,256]{1,0:T(8,128)(2,1)} %refs_1_.1, bf16[2048,256]{1,0:T(8,128)(2,1)} %refs_2_.1), custom_call_target="tpu_custom_call" | custom-call | tf_op jit(solution)/shard_map/pallas_call | solution.py:281
  43.7 3.9 %collective-permute-start.13 = (bf16[256,512]{1,0:T(8,128)(2,1)}, bf16[256,512]{1,0:T(8,128)(2,1)S(1)}, u32[]{:S(2)}, u32[]{:S(2)}) collective-permute-start(bf16[256,512]{1,0:T(8,128)(2,1)} %constant_dynamic-slice_fusion), channel_id=1, source_target_pairs={{0,4},{1,5},{2,6},{3,7},{4,0},{5,1},{6,2},{7,3},{8,12},{9,13},{10,... | collective-permute-start | bytes 786440 | tf_op jit(solution)/shard_map/ppermute | solution.py:56
  47.6 1.8 shard_map.120
  50.1 9.7 %collective-permute-done.13.refs_1_ = bf16[256,512]{1,0:T(8,128)(2,1)S(1)} collective-permute-done((bf16[256,512]{1,0:T(8,128)(2,1)}, bf16[256,512]{1,0:T(8,128)(2,1)S(1)}, u32[]{:S(2)}, u32[]{:S(2)}) %collective-permute-start.13) | collective-permute-done | bytes 262176 | tf_op jit(solution)/shard_map/ppermute | solution.py:56
  64.2 5.5 %collective-permute-done.10.refs_2_ = bf16[256,384]{1,0:T(8,128)(2,1)S(1)} collective-permute-done((bf16[256,384]{1,0:T(8,128)(2,1)S(1)}, bf16[256,384]{1,0:T(8,128)(2,1)S(1)}, u32[]{:S(2)}, u32[]{:S(2)}) %collective-permute-start.10) | collective-permute-done | bytes 196640 | tf_op jit(solution)/shard_map/ppermute | solution.py:61
  71.8 1.7 collective-permute-start.19
  75.0 3.1 %collective-permute-done.16.refs_5_ = bf16[128,384]{1,0:T(8,128)(2,1)S(1)} collective-permute-done((bf16[128,384]{1,0:T(8,128)(2,1)S(1)}, bf16[128,384]{1,0:T(8,128)(2,1)S(1)}, u32[]{:S(2)}, u32[]{:S(2)}) %collective-permute-start.16) | collective-permute-done | bytes 98336 | tf_op jit(solution)/shard_map/ppermute | solution.py:61
  92.7 2.1 shard_map.122
  98.9 9.0 %shard_map.123 = bf16[2048,128]{1,0:T(8,128)(2,1)} custom-call(s32[3]{0:T(128)} %pad_add_fusion.place_ref, f32[1,2048]{1,0:T(1,128)} %select_n.104.bias_ref, bf16[256,384]{1,0:T(8,128)(2,1)} %copy-done.3, bf16[256,384]{1,0:T(8,128)(2,1)} %copy-done.28, bf16[256,384]{1,0:T(8,128)(2,1)} %copy-done.26, bf16[256,384]{1,0:T(8,128)(2,1)} %copy-done.27, ...), custom_call_target="tpu_custom_call" | custom-call | flops 2147483648 | bytes 2105356 | tf_op jit(solution)/shard_map/pallas_call | solution.py:19
  107.9 3.6 %all-to-all-start = ((bf16[32,64,128]{2,1,0:T(8,128)(2,1)}), bf16[32,64,128]{2,1,0:T(8,128)(2,1)S(1)}, u32[]{:S(2)}, u32[]{:S(2)}) async-start(bf16[32,64,128]{2,1,0:T(8,128)(2,1)} %bitcast.42), calls=%async_computation | async-start | bytes 1048576 | tf_op jit(solution)/shard_map/all_to_all | solution.py:364
  116.7 11.6 %collective-permute-done.28.refs_7_ = bf16[384,512]{1,0:T(8,128)(2,1)} collective-permute-done((bf16[384,512]{1,0:T(8,128)(2,1)}, bf16[384,512]{1,0:T(8,128)(2,1)}, u32[]{:S(2)}, u32[]{:S(2)}) %collective-permute-start.28) | collective-permute-done | bytes 393248 | tf_op jit(solution)/shard_map/ppermute | solution.py:61
  131.6 7.5 %shard_map.124 = (f32[128,2048]{1,0:T(8,128)}, bf16[256,2048]{1,0:T(8,128)(2,1)}) custom-call(s32[3]{0:T(128)} %pad_add_fusion.place_ref, bf16[128,2048]{1,0:T(8,128)(2,1)} %copy-done, s32[128,1]{1,0:T(8,128)} %copy.20.live_ref, s32[1,128]{1,0:T(1,128)} %reshape.254.target_ref, bf16[1,2048]{1,0:T(2,128)(2,1)} %reshape.255.gain_ref, ...), custom_call_target="tpu_custom_call" | custom-call | flops 1207959552 | bytes 11539468 | tf_op jit(solution)/shard_map/pallas_call | solution.py:19
  139.1 32.8 %all_to_all.33 = bf16[32,8,2048]{2,1,0:T(8,128)(2,1)} all-to-all(bf16[32,8,2048]{2,1,0:T(8,128)(2,1)} %bitcast.41), channel_id=1, replica_groups=mesh['expert'=4,'head'=8] {'expert','head'}, dimensions={0} | all-to-all | bytes 2097152 | tf_op jit(solution)/shard_map/all_to_all | solution.py:383
  171.9 11.2 %shard_map.125 = bf16[256,2048]{1,0:T(8,128)(2,1)} custom-call(bf16[256,2048]{1,0:T(8,128)(2,1)} %bitcast.32, bf16[704,2048]{1,0:T(8,128)(2,1)} %bitcast.35, bf16[704,2048]{1,0:T(8,128)(2,1)} %bitcast.37, bf16[704,2048]{1,0:T(8,128)(2,1)} %bitcast.39, bf16[704,2048]{1,0:T(8,128)(2,1)} %collective-permute-done.2.refs_3_, ...), custom_call_target="tpu_custom_call" | custom-call | flops 4429185024 | bytes 19398656 | tf_op jit(solution)/shard_map/pallas_call | solution.py:19
  183.1 2.7 %all-to-all-start.2 = ((bf16[32,8,2048]{2,1,0:T(8,128)(2,1)}), bf16[32,8,2048]{2,1,0:T(8,128)(2,1)S(1)}, u32[]{:S(2)}, u32[]{:S(2)}) async-start(bf16[32,8,2048]{2,1,0:T(8,128)(2,1)} %bitcast.31), calls=%async_computation.2 | async-start | bytes 2097152 | tf_op jit(solution)/shard_map/all_to_all | solution.py:393
  186.5 26.8 %all-to-all-done.2 = bf16[32,8,2048]{2,1,0:T(8,128)(2,1)S(1)} async-done(((bf16[32,8,2048]{2,1,0:T(8,128)(2,1)}), bf16[32,8,2048]{2,1,0:T(8,128)(2,1)S(1)}, u32[]{:S(2)}, u32[]{:S(2)}) %all-to-all-start.2) | async-done | bytes 1048608 | tf_op jit(solution)/shard_map/all_to_all | solution.py:393
  214.3 2.7 %shard_map.126 = bf16[128,2048]{1,0:T(8,128)(2,1)} custom-call(f32[128,2048]{1,0:T(8,128)} %get-tuple-element.125.residual_ref, s32[128,1]{1,0:T(8,128)} %copy.21.target_ref, bf16[256,2048]{1,0:T(8,128)(2,1)} %bitcast.33), custom_call_target="tpu_custom_call" | custom-call | flops 134217728 | bytes 2621952 | tf_op jit(solution)/shard_map/pallas_call | solution.py:19
  (170 shorter events, 51.0 us)
Async XLA Ops:
  0.0 36.4 %collective-permute-start.2 = (bf16[704,2048]{1,0:T(8,128)(2,1)}, bf16[704,2048]{1,0:T(8,128)(2,1)}, u32[]{:S(2)}, u32[]{:S(2)}) collective-permute-start(bf16[704,2048]{1,0:T(8,128)(2,1)} %bitcast.34), channel_id=1, source_target_pairs={{0,1},{1,0},{2,3},{3,2},{4,5},{5,4},{6,7},{7,6},{8,9},{9,8},{10,11... | collective-permute-start | bytes 8650760 | tf_op jit(solution)/shard_map/ppermute | solution.py:36
  3.1 15.4 %collective-permute-start = (bf16[128,2048]{1,0:T(8,128)(2,1)S(1)}, bf16[128,2048]{1,0:T(8,128)(2,1)S(1)}, u32[]{:S(2)}, u32[]{:S(2)}) collective-permute-start(bf16[128,2048]{1,0:T(8,128)(2,1)S(1)} %maximum_select_fusion.refs_0_.own_ref), channel_id=1, source_target_pairs={{0,2},{2,0},{1,3},{3,1},{4,6},{6,4},{5,7},{7,5},{8,10},{10,8},{9,1... | collective-permute-start | bytes 1572872 | tf_op jit(solution)/shard_map/ppermute | solution.py:46
  5.8 13.5 %collective-permute-start.4 = (bf16[128,2048]{1,0:T(8,128)(2,1)S(1)}, bf16[128,2048]{1,0:T(8,128)(2,1)S(1)}, u32[]{:S(2)}, u32[]{:S(2)}) collective-permute-start(bf16[128,2048]{1,0:T(8,128)(2,1)S(1)} %maximum_select_fusion.refs_0_.own_ref), channel_id=1, source_target_pairs={{2,4},{4,2},{3,5},{5,3},{10,12},{12,10},{11,13},{13,11},{18,20},{2... | collective-permute-start | bytes 1572872 | tf_op jit(solution)/shard_map/ppermute | solution.py:46
  8.1 15.8 %collective-permute-start.12 = (bf16[256,512]{1,0:T(8,128)(2,1)}, bf16[256,512]{1,0:T(8,128)(2,1)S(1)}, u32[]{:S(2)}, u32[]{:S(2)}) collective-permute-start(bf16[256,512]{1,0:T(8,128)(2,1)} %constant_dynamic-slice_fusion), channel_id=1, source_target_pairs={{0,2},{1,3},{2,0},{3,1},{4,6},{5,7},{6,4},{7,5},{8,10},{9,11},{10,... | collective-permute-start | bytes 786440 | tf_op jit(solution)/shard_map/ppermute | solution.py:56
  12.5 50.2 %collective-permute-start.14 = (bf16[704,2048]{1,0:T(8,128)(2,1)}, bf16[704,2048]{1,0:T(8,128)(2,1)}, u32[]{:S(2)}, u32[]{:S(2)}) collective-permute-start(bf16[704,2048]{1,0:T(8,128)(2,1)} %bitcast.36), channel_id=1, source_target_pairs={{0,1},{1,0},{2,3},{3,2},{4,5},{5,4},{6,7},{7,6},{8,9},{9,8},{10,11... | collective-permute-start | bytes 8650760 | tf_op jit(solution)/shard_map/ppermute | solution.py:36
  19.2 17.1 %collective-permute-start.5 = (bf16[128,2048]{1,0:T(8,128)(2,1)S(1)}, bf16[128,2048]{1,0:T(8,128)(2,1)S(1)}, u32[]{:S(2)}, u32[]{:S(2)}) collective-permute-start(bf16[128,2048]{1,0:T(8,128)(2,1)S(1)} %collective-permute-done.4), channel_id=1, source_target_pairs={{2,0},{3,1},{4,6},{5,7},{10,8},{11,9},{12,14},{13,15},{18,16},{19,... | collective-permute-start | bytes 1572872 | tf_op jit(solution)/shard_map/ppermute | solution.py:51
  24.0 64.7 %collective-permute-start.23 = (bf16[704,2048]{1,0:T(8,128)(2,1)}, bf16[704,2048]{1,0:T(8,128)(2,1)}, u32[]{:S(2)}, u32[]{:S(2)}) collective-permute-start(bf16[704,2048]{1,0:T(8,128)(2,1)} %bitcast.38), channel_id=1, source_target_pairs={{0,1},{1,0},{2,3},{3,2},{4,5},{5,4},{6,7},{7,6},{8,9},{9,8},{10,11... | collective-permute-start | bytes 8650760 | tf_op jit(solution)/shard_map/ppermute | solution.py:36
  24.6 17.6 %collective-permute-start.7 = (bf16[128,2048]{1,0:T(8,128)(2,1)S(1)}, bf16[128,2048]{1,0:T(8,128)(2,1)S(1)}, u32[]{:S(2)}, u32[]{:S(2)}) collective-permute-start(bf16[128,2048]{1,0:T(8,128)(2,1)S(1)} %maximum_select_fusion.refs_0_.own_ref), channel_id=1, source_target_pairs={{0,1},{1,0},{2,3},{3,2},{4,5},{5,4},{6,7},{7,6},{8,9},{9,8},{10,11... | collective-permute-start | bytes 1572872 | tf_op jit(solution)/shard_map/ppermute | solution.py:36
  36.4 24.8 %collective-permute-start.6 = (bf16[128,2048]{1,0:T(8,128)(2,1)S(1)}, bf16[128,2048]{1,0:T(8,128)(2,1)S(1)}, u32[]{:S(2)}, u32[]{:S(2)}) collective-permute-start(bf16[128,2048]{1,0:T(8,128)(2,1)S(1)} %broadcast_select_fusion.1.refs_0_), channel_id=1, source_target_pairs={{0,1},{1,0},{2,3},{3,2},{4,5},{5,4},{6,7},{7,6},{8,9},{9,8},{10,11... | collective-permute-start | bytes 1572872 | tf_op jit(solution)/shard_map/ppermute | solution.py:36
  42.2 28.9 %collective-permute-start.3 = (bf16[128,2048]{1,0:T(8,128)(2,1)S(1)}, bf16[128,2048]{1,0:T(8,128)(2,1)S(1)}, u32[]{:S(2)}, u32[]{:S(2)}) collective-permute-start(bf16[128,2048]{1,0:T(8,128)(2,1)S(1)} %copy-done.10), channel_id=1, source_target_pairs={{2,0},{3,1},{4,6},{5,7},{10,8},{11,9},{12,14},{13,15},{18,16},{19,... | collective-permute-start | bytes 1572872 | tf_op jit(solution)/shard_map/ppermute | solution.py:51
  43.7 16.0 %collective-permute-start.13 = (bf16[256,512]{1,0:T(8,128)(2,1)}, bf16[256,512]{1,0:T(8,128)(2,1)S(1)}, u32[]{:S(2)}, u32[]{:S(2)}) collective-permute-start(bf16[256,512]{1,0:T(8,128)(2,1)} %constant_dynamic-slice_fusion), channel_id=1, source_target_pairs={{0,4},{1,5},{2,6},{3,7},{4,0},{5,1},{6,2},{7,3},{8,12},{9,13},{10,... | collective-permute-start | bytes 786440 | tf_op jit(solution)/shard_map/ppermute | solution.py:56
  71.3 43.9 %collective-permute-start.30 = (bf16[256,2048]{1,0:T(8,128)(2,1)S(1)}, bf16[256,2048]{1,0:T(8,128)(2,1)S(1)}, u32[]{:S(2)}, u32[]{:S(2)}) collective-permute-start(bf16[256,2048]{1,0:T(8,128)(2,1)S(1)} %copy-done.7), channel_id=1, source_target_pairs={{0,1},{1,0},{2,3},{3,2},{4,5},{5,4},{6,7},{7,6},{8,9},{9,8},{10,11... | collective-permute-start | bytes 3145736 | tf_op jit(solution)/shard_map/ppermute | solution.py:36
  71.8 15.4 %collective-permute-start.19 = (bf16[256,512]{1,0:T(8,128)(2,1)}, bf16[256,512]{1,0:T(8,128)(2,1)S(1)}, u32[]{:S(2)}, u32[]{:S(2)}) collective-permute-start(bf16[256,512]{1,0:T(8,128)(2,1)} %constant_dynamic-slice_fusion), channel_id=1, source_target_pairs={{0,6},{1,7},{2,4},{3,5},{4,2},{5,3},{6,0},{7,1},{8,14},{9,15},{10,... | collective-permute-start | bytes 786440 | tf_op jit(solution)/shard_map/ppermute | solution.py:56
  94.8 16.7 %collective-permute-start.24 = (bf16[384,512]{1,0:T(8,128)(2,1)}, bf16[384,512]{1,0:T(8,128)(2,1)}, u32[]{:S(2)}, u32[]{:S(2)}) collective-permute-start(bf16[384,512]{1,0:T(8,128)(2,1)} %get-tuple-element.119.refs_1_), channel_id=1, source_target_pairs={{0,8},{8,0},{16,24},{24,16},{1,9},{9,1},{17,25},{25,17},{2,10},{10... | collective-permute-start | bytes 1179656 | tf_op jit(solution)/shard_map/ppermute | solution.py:61
  95.3 16.8 %collective-permute-start.26 = (bf16[384,512]{1,0:T(8,128)(2,1)}, bf16[384,512]{1,0:T(8,128)(2,1)}, u32[]{:S(2)}, u32[]{:S(2)}) collective-permute-start(bf16[384,512]{1,0:T(8,128)(2,1)} %get-tuple-element.119.refs_1_), channel_id=1, source_target_pairs={{0,16},{8,24},{16,0},{24,8},{1,17},{9,25},{17,1},{25,9},{2,18},{10... | collective-permute-start | bytes 1179656 | tf_op jit(solution)/shard_map/ppermute | solution.py:61
  96.8 14.8 %collective-permute-start.25 = (bf16[384,512]{1,0:T(8,128)(2,1)}, bf16[384,512]{1,0:T(8,128)(2,1)}, u32[]{:S(2)}, u32[]{:S(2)}) collective-permute-start(bf16[384,512]{1,0:T(8,128)(2,1)} %get-tuple-element.120.refs_2_), channel_id=1, source_target_pairs={{0,8},{8,0},{16,24},{24,16},{1,9},{9,1},{17,25},{25,17},{2,10},{10... | collective-permute-start | bytes 1179656 | tf_op jit(solution)/shard_map/ppermute | solution.py:61
  98.3 13.8 %collective-permute-start.27 = (bf16[384,512]{1,0:T(8,128)(2,1)}, bf16[384,512]{1,0:T(8,128)(2,1)}, u32[]{:S(2)}, u32[]{:S(2)}) collective-permute-start(bf16[384,512]{1,0:T(8,128)(2,1)} %get-tuple-element.120.refs_2_), channel_id=1, source_target_pairs={{0,16},{8,24},{16,0},{24,8},{1,17},{9,25},{17,1},{25,9},{2,18},{10... | collective-permute-start | bytes 1179656 | tf_op jit(solution)/shard_map/ppermute | solution.py:61
  107.9 22.4 %all-to-all-start = ((bf16[32,64,128]{2,1,0:T(8,128)(2,1)}), bf16[32,64,128]{2,1,0:T(8,128)(2,1)S(1)}, u32[]{:S(2)}, u32[]{:S(2)}) async-start(bf16[32,64,128]{2,1,0:T(8,128)(2,1)} %bitcast.42), calls=%async_computation | async-start | bytes 1048576 | tf_op jit(solution)/shard_map/all_to_all | solution.py:364
  112.1 16.2 %collective-permute-start.28 = (bf16[384,512]{1,0:T(8,128)(2,1)}, bf16[384,512]{1,0:T(8,128)(2,1)}, u32[]{:S(2)}, u32[]{:S(2)}) collective-permute-start(bf16[384,512]{1,0:T(8,128)(2,1)} %collective-permute-done.26.refs_5_), channel_id=1, source_target_pairs={{0,8},{8,0},{16,24},{24,16},{1,9},{9,1},{17,25},{25,17},{2,10},{10... | collective-permute-start | bytes 1179656 | tf_op jit(solution)/shard_map/ppermute | solution.py:61
  113.7 15.2 %collective-permute-start.29 = (bf16[384,512]{1,0:T(8,128)(2,1)}, bf16[384,512]{1,0:T(8,128)(2,1)}, u32[]{:S(2)}, u32[]{:S(2)}) collective-permute-start(bf16[384,512]{1,0:T(8,128)(2,1)} %collective-permute-done.25.refs_4_), channel_id=1, source_target_pairs={{0,16},{8,24},{16,0},{24,8},{1,17},{9,25},{17,1},{25,9},{2,18},{10... | collective-permute-start | bytes 1179656 | tf_op jit(solution)/shard_map/ppermute | solution.py:61
  115.2 13.7 %collective-permute-start.33 = (bf16[384,512]{1,0:T(8,128)(2,1)}, bf16[384,512]{1,0:T(8,128)(2,1)S(1)}, u32[]{:S(2)}, u32[]{:S(2)}) collective-permute-start(bf16[384,512]{1,0:T(8,128)(2,1)} %collective-permute-done.24.refs_3_), channel_id=1, source_target_pairs={{0,1},{1,0},{2,3},{3,2},{4,5},{5,4},{6,7},{7,6},{8,9},{9,8},{10,11... | collective-permute-start | bytes 1179656 | tf_op jit(solution)/shard_map/ppermute | solution.py:36
  115.2 14.9 %collective-permute-start.34 = (bf16[384,512]{1,0:T(8,128)(2,1)}, bf16[384,512]{1,0:T(8,128)(2,1)S(1)}, u32[]{:S(2)}, u32[]{:S(2)}) collective-permute-start(bf16[384,512]{1,0:T(8,128)(2,1)} %collective-permute-done.25.refs_4_), channel_id=1, source_target_pairs={{0,1},{1,0},{2,3},{3,2},{4,5},{5,4},{6,7},{7,6},{8,9},{9,8},{10,11... | collective-permute-start | bytes 1179656 | tf_op jit(solution)/shard_map/ppermute | solution.py:36
  116.0 14.1 %collective-permute-start.35 = (bf16[384,512]{1,0:T(8,128)(2,1)}, bf16[384,512]{1,0:T(8,128)(2,1)S(1)}, u32[]{:S(2)}, u32[]{:S(2)}) collective-permute-start(bf16[384,512]{1,0:T(8,128)(2,1)} %collective-permute-done.26.refs_5_), channel_id=1, source_target_pairs={{0,1},{1,0},{2,3},{3,2},{4,5},{5,4},{6,7},{7,6},{8,9},{9,8},{10,11... | collective-permute-start | bytes 1179656 | tf_op jit(solution)/shard_map/ppermute | solution.py:36
  183.1 30.3 %all-to-all-start.2 = ((bf16[32,8,2048]{2,1,0:T(8,128)(2,1)}), bf16[32,8,2048]{2,1,0:T(8,128)(2,1)S(1)}, u32[]{:S(2)}, u32[]{:S(2)}) async-start(bf16[32,8,2048]{2,1,0:T(8,128)(2,1)} %bitcast.31), calls=%async_computation.2 | async-start | bytes 2097152 | tf_op jit(solution)/shard_map/all_to_all | solution.py:393
  (52 other events, 481.1 us)

commit v3 on v2

--- a/solution.py
+++ b/solution.py
@@ -115,30 +115,25 @@
 
 
 def attend_body(block, place_ref, bias_ref, *refs):
-    early, middle, late = refs[:4], refs[4:8], refs[8:12]
-    out_ref, (keys, values) = refs[12], refs[13:]
+    early, late = refs[:4], refs[4:8]
+    out_ref, (keys, values) = refs[8], refs[9:]
     spot, place, core = place_ref[0], place_ref[1], place_ref[2]
     planes = 4
     half = block // 2
     for source in range(4):
-        parts = (
-            early[source][pl.ds(0, block), :],
-            early[source][pl.ds(block, block), :],
-            middle[source][...],
-            late[source][...],
-        )
         for slot in range(planes):
             span = pl.ds((slot * 4 + source) * block, block)
-            keys[span, :] = parts[slot][:, DH : 2 * DH]
-            values[span, :] = parts[slot][:, 2 * DH :]
+            rows = pl.ds(slot % 2 * block, block)
+            part = (early, late)[slot // 2][source]
+            keys[span, :] = part[rows, pl.ds(DH, DH)]
+            values[span, :] = part[rows, pl.ds(2 * DH, DH)]
     scale = 1.0 / math.sqrt(DH) * math.log2(math.e)
     third = jnp.where(place < 2, 2, 1)
     fourth = jnp.where(place < 2, 3, 0)
 
     def queries(slot, source):
-        if slot < 2:
-            return early[source][pl.ds(slot * block, block), pl.ds(0, DH)]
-        return (middle, late)[slot - 2][source][:, pl.ds(0, DH)]
+        rows = pl.ds(slot % 2 * block, block)
+        return (early, late)[slot // 2][source][rows, pl.ds(0, DH)]
 
     for slot, plane in enumerate((place, place ^ 1, third, fourth)):
         for first in (0, 2):
@@ -237,16 +232,19 @@
     out_ref[...] = total.astype(jnp.bfloat16)
 
 
-def finish_body(residual_ref, target_ref, blocks_ref, out_ref):
-    slots = blocks_ref.shape[0]
-    rows = residual_ref.shape[0]
+def finish_body(residual_ref, target_ref, blocks_ref, place_ref, out_ref):
+    slots, rows = blocks_ref.shape[0], residual_ref.shape[0]
     chosen = target_ref[...] == lax.broadcasted_iota(jnp.int32, (rows, slots), 1)
     expert_out = jnp.dot(
         chosen.astype(jnp.float32).astype(jnp.bfloat16),
         blocks_ref[...],
         preferred_element_type=jnp.float32,
     )
-    out_ref[...] = (residual_ref[...] + expert_out).astype(jnp.bfloat16)
+    updated = residual_ref[...] + expert_out
+    mine, other = updated[: rows // 2], updated[rows // 2 :]
+    in_order = place_ref[0] < 2
+    out_ref[:, 0, :] = jnp.where(in_order, mine, other).astype(jnp.bfloat16)
+    out_ref[:, 1, :] = jnp.where(in_order, other, mine).astype(jnp.bfloat16)
 
 
 def paired_shards(
@@ -284,6 +282,9 @@
         in_specs=[SMEM] + [VMEM] * 3,
         out_specs=VMEM,
         compiler_params=pltpu.CompilerParams(vmem_limit_bytes=56 * 1024 * 1024),
+        cost_estimate=pl.CostEstimate(
+            flops=0, bytes_accessed=24 * w_query.size, transcendentals=0
+        ),
     )(parity.reshape(1).astype(jnp.int32), w_query, w_key, w_value)
 
     def spread(outs):
@@ -315,44 +316,43 @@
     beside = neighbours(own, 0)
     inner = neighbours(own, 1)
     beside_too = swap_cores(beside)
-    outer = outwards(inner)
-    inner_far = neighbours(beside, 1)
     quarter = width // 4
     part = lax.dynamic_slice_in_dim(w_out, spot * quarter, quarter, 1)
     parts = [across_z(part, bits) for bits in range(1, planes)]
     small = (bias, where, live, target, target_column, gain)
     halves = [w_gate[0], w_up[0], w_down[0]]
     others = [swap_cores(w) for w in halves]
-    inner_far, small, weight, others[0] = lax.optimization_barrier(
-        (inner_far, small, weight, others[0])
+    inner, small, weight, others[0], parts[0] = lax.optimization_barrier(
+        (inner, small, weight, others[0], parts[0])
     )
     bias, where, live, target, target_column, gain = small
+    outer = outwards(inner)
+    inner_far = neighbours(beside, 1)
     early_out = project([(own, swap_cores(own)), (beside, beside_too)], weight)
     early = spread(early_out)
     outer_far = outwards(inner_far)
     third = jnp.where(inside, inner, outer)
-    middle_out = project([(third, swap_cores(third))], weight)
-    outer_far, middle_out, early, parts[0], parts[1], others[1] = lax.optimization_barrier(
-        (outer_far, middle_out, early, parts[0], parts[1], others[1])
-    )
-    middle = spread(middle_out)
+    third_too = swap_cores(third)
+    outer_far, third_too, others[1] = lax.optimization_barrier(
+        (outer_far, third_too, others[1])
+    )
     fourth = jnp.where(inside, inner_far, outer_far)
-    late_out = project([(fourth, swap_cores(fourth))], weight)
-    late_out, middle = lax.optimization_barrier((late_out, middle))
+    late_out = project([(third, third_too), (fourth, swap_cores(fourth))], weight)
+    late_out, early, parts[1] = lax.optimization_barrier((late_out, early, parts[1]))
     late = spread(late_out)
 
     parts, late, others[2] = lax.optimization_barrier((parts, late, others[2]))
     expert_weights = halves + others
     far = stack(parts)
     far, late = lax.optimization_barrier((far, late))
-    shared = early + middle + late
+    shared = early + late
     fars = [[in_plane(half, bits) for half in far] for bits in (1, 2)]
     everyone = ("expert", "head")
     attended = local_call(
         functools.partial(attend_body, block),
         [shape_of((count, DH))],
         [where, bias] + shared,
-        [SMEM] + [VMEM] * 13,
+        [SMEM] + [VMEM] * 9,
         4 * count * count * DH,
         [pltpu.VMEM((count, DH), jnp.bfloat16)] * 2,
         grant=60,
@@ -391,18 +391,14 @@
         grant=60,
     )[0]
     gathered = lax.all_to_all(computed, everyone, 0, 0, tiled=True)
-    updated = local_call(
+    return local_call(
         finish_body,
-        [shape_of((rows_dev, width))],
-        [residual, target_column, gathered],
-        [VMEM] * 3,
+        [shape_of((cells, tables, width))],
+        [residual, target_column, gathered, where],
+        [VMEM] * 3 + [SMEM],
         2 * rows_dev * width * slots,
-        grant=60,
+        grant=48,
     )[0]
-    first, second = updated[:cells], updated[cells:]
-    return jnp.stack(
-        [jnp.where(mine == 0, first, second), jnp.where(mine == 0, second, first)], axis=1
-    )
 
 
 def from_partner(block, axis, bit):

time: 220 us -> 217 us (0.986)
  starting transfers between devices: 45.8 us -> 36.7 us
  waiting for transfers between devices: 85.4 us -> 94.2 us
  local copies, waits for them, and re-layouts: 13.3 us -> 10.6 us
    ppermute x2, waiting for transfers between devices: 11.1 us -> 22.3 us  [outwards(): return lax.ppermute(block, 'head', route)]
    ppermute x3, starting transfers between devices: 10 us -> 3.15 us  [across_z(): lax.ppermute(block, 'head', [(h, h ^ 2 * bits) for h in range(count)])]
    ppermute x15 -> x12, starting transfers between devices: 18.5 us -> 14.2 us  [in_plane(): return lax.ppermute(block, 'expert', [(e, e ^ bits) for e in range(count)])]
    ppermute x3, starting transfers between devices: 4.04 us -> 7.61 us  [neighbours(): return lax.ppermute(block, 'head', route)]
    ppermute x15 -> x12, waiting for transfers between devices: 28.6 us -> 27.3 us  [in_plane(): return lax.ppermute(block, 'expert', [(e, e ^ bits) for e in range(count)])]
    pallas_call x8 -> x7, Pallas kernels: 36.3 us -> 36.5 us  [local_call(): pl.pallas_call(body, out_shape=outs, in_specs=specs, out_specs=[VMEM] * l...]
  transfers between devices with their start and end apart: 41 -> 38, of which waited for: 19 -> 15; matrix products, arithmetic and copies ran while one was open for 5% -> 6% of each run, Pallas kernels for 8% -> 8%
where the time goes in v3:
time: 217 us
  waiting for transfers between devices  94.2 us (43%)
  Pallas kernels  38.9 us (18%)
  starting transfers between devices  36.7 us (17%)
  blocking collectives  32 us (15%)
  local copies, waits for them, and re-layouts  10.6 us (5%)
  other arithmetic  3.74 us (2%)
    pallas_call x7, Pallas kernels, local_call(): pl.pallas_call(body, out_shape=outs, in_specs=specs, out_specs=[VMEM] * l...  36.5 us
    all_to_all x1, blocking collectives, paired_shards(): received = lax.all_to_all(send_rows, everyone, 0, 0, tiled=True)  32 us
    all_to_all x1, waiting for transfers between devices, paired_shards(): gathered = lax.all_to_all(computed, everyone, 0, 0, tiled=True)  27.5 us
    ppermute x12, waiting for transfers between devices, in_plane(): return lax.ppermute(block, 'expert', [(e, e ^ bits) for e in range(count)])  27.3 us
    ppermute x2, waiting for transfers between devices, outwards(): return lax.ppermute(block, 'head', route)  22.3 us
    ppermute x12, starting transfers between devices, in_plane(): return lax.ppermute(block, 'expert', [(e, e ^ bits) for e in range(count)])  14.2 us
    ppermute x3, waiting for transfers between devices, across_z(): lax.ppermute(block, 'head', [(h, h ^ 2 * bits) for h in range(count)])  12 us
    ppermute x3, starting transfers between devices, neighbours(): return lax.ppermute(block, 'head', route)  7.61 us
  transfers between devices with their start and end apart: 38, of which 15 were waited for; matrix products, arithmetic and copies ran while one was open for 6% of the time, Pallas kernels for 8%

profile of v3, /device:TPU:0, one launch (start us, length us, event | category | flops | bytes accessed | tf_op | source)
XLA Modules:
  0.0 216.5 jit_solution(17072316021226201680)
XLA Ops:
  0.5 2.1 fusion.1
  5.4 4.7 %collective-permute-start.4 = (bf16[128,2048]{1,0:T(8,128)(2,1)}, bf16[128,2048]{1,0:T(8,128)(2,1)}, u32[]{:S(2)}, u32[]{:S(2)}) collective-permute-start(bf16[128,2048]{1,0:T(8,128)(2,1)} %maximum_select_fusion.refs_0_.own_ref), channel_id=1, source_target_pairs={{0,2},{2,0},{1,3},{3,1},{4,6},{6,4},{5,7},{7,5},{8,10},{10,8},{9,1... | collective-permute-start | bytes 1572872 | tf_op jit(solution)/shard_map/ppermute | solution.py:46
  16.2 2.4 %shard_map.118.refs_4_ = bf16[2048,768]{1,0:T(8,128)(2,1)S(1)} custom-call(s32[1]{0:T(128)} %bitcast.13.place_ref, bf16[2048,256]{1,0:T(8,128)(2,1)} %refs_0_.2, bf16[2048,256]{1,0:T(8,128)(2,1)} %refs_1_.1, bf16[2048,256]{1,0:T(8,128)(2,1)} %refs_2_.1), custom_call_target="tpu_custom_call" | custom-call | bytes 12582912 | tf_op jit(solution)/shard_map/pallas_call | solution.py:279
  19.2 3.9 %collective-permute-done.4.refs_2_ = bf16[128,2048]{1,0:T(8,128)(2,1)} collective-permute-done((bf16[128,2048]{1,0:T(8,128)(2,1)}, bf16[128,2048]{1,0:T(8,128)(2,1)}, u32[]{:S(2)}, u32[]{:S(2)}) %collective-permute-start.4) | collective-permute-done | bytes 524320 | tf_op jit(solution)/shard_map/ppermute | solution.py:46
  24.5 3.6 %collective-permute-done.2.refs_0_ = bf16[256,512]{1,0:T(8,128)(2,1)S(1)} collective-permute-done((bf16[256,512]{1,0:T(8,128)(2,1)}, bf16[256,512]{1,0:T(8,128)(2,1)S(1)}, u32[]{:S(2)}, u32[]{:S(2)}) %collective-permute-start.2) | collective-permute-done | bytes 262176 | tf_op jit(solution)/shard_map/ppermute | solution.py:56
  31.1 14.2 %collective-permute-done.3 = bf16[128,2048]{1,0:T(8,128)(2,1)} collective-permute-done((bf16[128,2048]{1,0:T(8,128)(2,1)}, bf16[128,2048]{1,0:T(8,128)(2,1)}, u32[]{:S(2)}, u32[]{:S(2)}) %collective-permute-start.3) | collective-permute-done | bytes 524320 | tf_op jit(solution)/shard_map/ppermute | solution.py:51
  46.9 8.2 %collective-permute-done.6 = bf16[128,2048]{1,0:T(8,128)(2,1)S(1)} collective-permute-done((bf16[128,2048]{1,0:T(8,128)(2,1)}, bf16[128,2048]{1,0:T(8,128)(2,1)S(1)}, u32[]{:S(2)}, u32[]{:S(2)}) %collective-permute-start.6) | collective-permute-done | bytes 524320 | tf_op jit(solution)/shard_map/ppermute | solution.py:51
  57.2 3.0 %shard_map.120 = (bf16[256,384]{1,0:T(8,128)(2,1)S(1)}, bf16[256,384]{1,0:T(8,128)(2,1)S(1)}, bf16[256,384]{1,0:T(8,128)(2,1)S(1)}, bf16[256,384]{1,0:T(8,128)(2,1)S(1)}) custom-call(bf16[128,2048]{1,0:T(8,128)(2,1)} %maximum_select_fusion.refs_0_.own_ref, bf16[128,2048]{1,0:T(8,128)(2,1)S(1)} %collective-permute-done.10.refs_1_, ...), custom_call_target="tpu_custom_call" | custom-call | flops 1610612736 | bytes 6029312 | tf_op jit(solution)/shard_map/pallas_call | solution.py:19
  62.3 8.4 %collective-permute-done.15.refs_1_ = bf16[256,512]{1,0:T(8,128)(2,1)S(1)} collective-permute-done((bf16[256,512]{1,0:T(8,128)(2,1)}, bf16[256,512]{1,0:T(8,128)(2,1)S(1)}, u32[]{:S(2)}, u32[]{:S(2)}) %collective-permute-start.15) | collective-permute-done | bytes 262176 | tf_op jit(solution)/shard_map/ppermute | solution.py:56
  70.7 2.0 collective-permute-start.16
  75.6 1.8 shard_map.119
  78.1 5.2 %collective-permute-done.13.refs_2_ = bf16[256,384]{1,0:T(8,128)(2,1)S(1)} collective-permute-done((bf16[256,384]{1,0:T(8,128)(2,1)S(1)}, bf16[256,384]{1,0:T(8,128)(2,1)S(1)}, u32[]{:S(2)}, u32[]{:S(2)}) %collective-permute-start.13) | collective-permute-done | bytes 196640 | tf_op jit(solution)/shard_map/ppermute | solution.py:61
  86.9 4.1 %collective-permute-done.17.refs_5_ = bf16[256,384]{1,0:T(8,128)(2,1)S(1)} collective-permute-done((bf16[256,384]{1,0:T(8,128)(2,1)S(1)}, bf16[256,384]{1,0:T(8,128)(2,1)S(1)}, u32[]{:S(2)}, u32[]{:S(2)}) %collective-permute-start.17) | collective-permute-done | bytes 196640 | tf_op jit(solution)/shard_map/ppermute | solution.py:61
  91.0 3.6 %collective-permute-done.18.refs_6_ = bf16[256,384]{1,0:T(8,128)(2,1)S(1)} collective-permute-done((bf16[256,384]{1,0:T(8,128)(2,1)S(1)}, bf16[256,384]{1,0:T(8,128)(2,1)S(1)}, u32[]{:S(2)}, u32[]{:S(2)}) %collective-permute-start.18) | collective-permute-done | bytes 196640 | tf_op jit(solution)/shard_map/ppermute | solution.py:61
  94.7 2.2 %shard_map.121 = (bf16[384,512]{1,0:T(8,128)(2,1)}, bf16[384,512]{1,0:T(8,128)(2,1)}) custom-call(bf16[256,512]{1,0:T(8,128)(2,1)} %copy-done.17, bf16[256,512]{1,0:T(8,128)(2,1)} %copy-done.18, bf16[256,512]{1,0:T(8,128)(2,1)} %copy-done.19), custom_call_target="tpu_custom_call" | custom-call | bytes 1572864 | tf_op jit(solution)/shard_map/pallas_call | solution.py:19
  100.9 9.1 %shard_map.122 = bf16[2048,128]{1,0:T(8,128)(2,1)} custom-call(s32[3]{0:T(128)} %pad_add_fusion.place_ref, f32[1,2048]{1,0:T(1,128)} %select_n.91.bias_ref, bf16[256,384]{1,0:T(8,128)(2,1)} %copy-done.2, bf16[256,384]{1,0:T(8,128)(2,1)} %copy-done.23, bf16[256,384]{1,0:T(8,128)(2,1)} %copy-done.24, bf16[256,384]{1,0:T(8,128)(2,1)} %copy-done.25, ...), custom_call_target="tpu_custom_call" | custom-call | flops 2147483648 | bytes 2105356 | tf_op jit(solution)/shard_map/pallas_call | solution.py:19
  109.9 3.2 %all-to-all-start = ((bf16[32,64,128]{2,1,0:T(8,128)(2,1)}), bf16[32,64,128]{2,1,0:T(8,128)(2,1)S(1)}, u32[]{:S(2)}, u32[]{:S(2)}) async-start(bf16[32,64,128]{2,1,0:T(8,128)(2,1)} %bitcast.34), calls=%async_computation | async-start | bytes 1048576 | tf_op jit(solution)/shard_map/all_to_all | solution.py:364
  117.6 12.4 %collective-permute-done.25.refs_7_ = bf16[384,512]{1,0:T(8,128)(2,1)} collective-permute-done((bf16[384,512]{1,0:T(8,128)(2,1)S(1)}, bf16[384,512]{1,0:T(8,128)(2,1)}, u32[]{:S(2)}, u32[]{:S(2)}) %collective-permute-start.25) | collective-permute-done | bytes 393248 | tf_op jit(solution)/shard_map/ppermute | solution.py:61
  133.6 7.5 %shard_map.123 = (f32[128,2048]{1,0:T(8,128)}, bf16[256,2048]{1,0:T(8,128)(2,1)}) custom-call(s32[3]{0:T(128)} %pad_add_fusion.place_ref, bf16[128,2048]{1,0:T(8,128)(2,1)} %maximum_select_fusion.refs_0_.own_ref, s32[128,1]{1,0:T(8,128)} %copy.19.live_ref, s32[1,128]{1,0:T(1,128)} %reshape.254.target_ref, bf16[1,2048]{1,0:T(2,128)(2,1)} %reshape.255.gain_ref, ...), custom_call_target="tpu_custom_call" | custom-call | flops 1207959552 | bytes 11539468 | tf_op jit(solution)/shard_map/pallas_call | solution.py:19
  141.1 32.0 %all_to_all.33 = bf16[32,8,2048]{2,1,0:T(8,128)(2,1)} all-to-all(bf16[32,8,2048]{2,1,0:T(8,128)(2,1)} %bitcast.33), channel_id=1, replica_groups=mesh['expert'=4,'head'=8] {'expert','head'}, dimensions={0} | all-to-all | bytes 2097152 | tf_op jit(solution)/shard_map/all_to_all | solution.py:383
  173.1 11.2 %shard_map.124 = bf16[256,2048]{1,0:T(8,128)(2,1)} custom-call(bf16[256,2048]{1,0:T(8,128)(2,1)} %bitcast.29, bf16[704,2048]{1,0:T(8,128)(2,1)} %bitcast.31, bf16[704,2048]{1,0:T(8,128)(2,1)} %bitcast.15.refs_1_, bf16[704,2048]{1,0:T(8,128)(2,1)} %bitcast.16.refs_2_, bf16[704,2048]{1,0:T(8,128)(2,1)} %collective-permute-done.1.refs_3_, ...), custom_call_target="tpu_custom_call" | custom-call | flops 4429185024 | bytes 19398656 | tf_op jit(solution)/shard_map/pallas_call | solution.py:19
  184.3 2.8 %all-to-all-start.2 = ((bf16[32,8,2048]{2,1,0:T(8,128)(2,1)}), bf16[32,8,2048]{2,1,0:T(8,128)(2,1)S(1)}, u32[]{:S(2)}, u32[]{:S(2)}) async-start(bf16[32,8,2048]{2,1,0:T(8,128)(2,1)} %bitcast.28), calls=%async_computation.2 | async-start | bytes 2097152 | tf_op jit(solution)/shard_map/all_to_all | solution.py:393
  187.2 27.5 %all-to-all-done.2 = bf16[32,8,2048]{2,1,0:T(8,128)(2,1)S(1)} async-done(((bf16[32,8,2048]{2,1,0:T(8,128)(2,1)}), bf16[32,8,2048]{2,1,0:T(8,128)(2,1)S(1)}, u32[]{:S(2)}, u32[]{:S(2)}) %all-to-all-start.2) | async-done | bytes 1048608 | tf_op jit(solution)/shard_map/all_to_all | solution.py:393
  214.7 1.8 shard_map.125
  (147 shorter events, 39.5 us)
Async XLA Ops:
  0.0 28.2 %collective-permute-start.1 = (bf16[704,2048]{1,0:T(8,128)(2,1)}, bf16[704,2048]{1,0:T(8,128)(2,1)}, u32[]{:S(2)}, u32[]{:S(2)}) collective-permute-start(bf16[704,2048]{1,0:T(8,128)(2,1)} %bitcast.30), channel_id=1, source_target_pairs={{0,1},{1,0},{2,3},{3,2},{4,5},{5,4},{6,7},{7,6},{8,9},{9,8},{10,11... | collective-permute-start | bytes 8650760 | tf_op jit(solution)/shard_map/ppermute | solution.py:36
  3.9 24.3 %collective-permute-start = (bf16[128,2048]{1,0:T(8,128)(2,1)}, bf16[128,2048]{1,0:T(8,128)(2,1)}, u32[]{:S(2)}, u32[]{:S(2)}) collective-permute-start(bf16[128,2048]{1,0:T(8,128)(2,1)} %maximum_select_fusion.refs_0_.own_ref), channel_id=1, source_target_pairs={{2,4},{4,2},{3,5},{5,3},{10,12},{12,10},{11,13},{13,11},{18,20},{2... | collective-permute-start | bytes 1572872 | tf_op jit(solution)/shard_map/ppermute | solution.py:46
  5.4 17.7 %collective-permute-start.4 = (bf16[128,2048]{1,0:T(8,128)(2,1)}, bf16[128,2048]{1,0:T(8,128)(2,1)}, u32[]{:S(2)}, u32[]{:S(2)}) collective-permute-start(bf16[128,2048]{1,0:T(8,128)(2,1)} %maximum_select_fusion.refs_0_.own_ref), channel_id=1, source_target_pairs={{0,2},{2,0},{1,3},{3,1},{4,6},{6,4},{5,7},{7,5},{8,10},{10,8},{9,1... | collective-permute-start | bytes 1572872 | tf_op jit(solution)/shard_map/ppermute | solution.py:46
  11.7 16.5 %collective-permute-start.2 = (bf16[256,512]{1,0:T(8,128)(2,1)}, bf16[256,512]{1,0:T(8,128)(2,1)S(1)}, u32[]{:S(2)}, u32[]{:S(2)}) collective-permute-start(bf16[256,512]{1,0:T(8,128)(2,1)} %constant_dynamic-slice_fusion), channel_id=1, source_target_pairs={{0,2},{1,3},{2,0},{3,1},{4,6},{5,7},{6,4},{7,5},{8,10},{9,11},{10,... | collective-permute-start | bytes 786440 | tf_op jit(solution)/shard_map/ppermute | solution.py:56
  11.7 43.3 %collective-permute-start.8 = (bf16[704,2048]{1,0:T(8,128)(2,1)}, bf16[704,2048]{1,0:T(8,128)(2,1)}, u32[]{:S(2)}, u32[]{:S(2)}) collective-permute-start(bf16[704,2048]{1,0:T(8,128)(2,1)} %bitcast.15.refs_1_), channel_id=1, source_target_pairs={{0,1},{1,0},{2,3},{3,2},{4,5},{5,4},{6,7},{7,6},{8,9},{9,8},{10,11... | collective-permute-start | bytes 8650760 | tf_op jit(solution)/shard_map/ppermute | solution.py:36
  28.2 17.0 %collective-permute-start.3 = (bf16[128,2048]{1,0:T(8,128)(2,1)}, bf16[128,2048]{1,0:T(8,128)(2,1)}, u32[]{:S(2)}, u32[]{:S(2)}) collective-permute-start(bf16[128,2048]{1,0:T(8,128)(2,1)} %collective-permute-done), channel_id=1, source_target_pairs={{2,0},{3,1},{4,6},{5,7},{10,8},{11,9},{12,14},{13,15},{18,16},{19,... | collective-permute-start | bytes 1572872 | tf_op jit(solution)/shard_map/ppermute | solution.py:51
  29.5 57.4 %collective-permute-start.20 = (bf16[704,2048]{1,0:T(8,128)(2,1)}, bf16[704,2048]{1,0:T(8,128)(2,1)}, u32[]{:S(2)}, u32[]{:S(2)}) collective-permute-start(bf16[704,2048]{1,0:T(8,128)(2,1)} %bitcast.16.refs_2_), channel_id=1, source_target_pairs={{0,1},{1,0},{2,3},{3,2},{4,5},{5,4},{6,7},{7,6},{8,9},{9,8},{10,11... | collective-permute-start | bytes 8650760 | tf_op jit(solution)/shard_map/ppermute | solution.py:36
  29.6 25.5 %collective-permute-start.6 = (bf16[128,2048]{1,0:T(8,128)(2,1)}, bf16[128,2048]{1,0:T(8,128)(2,1)S(1)}, u32[]{:S(2)}, u32[]{:S(2)}) collective-permute-start(bf16[128,2048]{1,0:T(8,128)(2,1)} %collective-permute-done.5), channel_id=1, source_target_pairs={{2,0},{3,1},{4,6},{5,7},{10,8},{11,9},{12,14},{13,15},{18,16},{19,... | collective-permute-start | bytes 1572872 | tf_op jit(solution)/shard_map/ppermute | solution.py:51
  55.1 19.1 %collective-permute-start.9 = (bf16[128,2048]{1,0:T(8,128)(2,1)S(1)}, bf16[128,2048]{1,0:T(8,128)(2,1)S(1)}, u32[]{:S(2)}, u32[]{:S(2)}) collective-permute-start(bf16[128,2048]{1,0:T(8,128)(2,1)S(1)} %broadcast_select_fusion.refs_2_), channel_id=1, source_target_pairs={{0,1},{1,0},{2,3},{3,2},{4,5},{5,4},{6,7},{7,6},{8,9},{9,8},{10,11... | collective-permute-start | bytes 1572872 | tf_op jit(solution)/shard_map/ppermute | solution.py:36
  55.7 15.0 %collective-permute-start.15 = (bf16[256,512]{1,0:T(8,128)(2,1)}, bf16[256,512]{1,0:T(8,128)(2,1)S(1)}, u32[]{:S(2)}, u32[]{:S(2)}) collective-permute-start(bf16[256,512]{1,0:T(8,128)(2,1)} %constant_dynamic-slice_fusion), channel_id=1, source_target_pairs={{0,4},{1,5},{2,6},{3,7},{4,0},{5,1},{6,2},{7,3},{8,12},{9,13},{10,... | collective-permute-start | bytes 786440 | tf_op jit(solution)/shard_map/ppermute | solution.py:56
  56.9 60.1 %collective-permute-start.27 = (bf16[256,2048]{1,0:T(8,128)(2,1)}, bf16[256,2048]{1,0:T(8,128)(2,1)}, u32[]{:S(2)}, u32[]{:S(2)}) collective-permute-start(bf16[256,2048]{1,0:T(8,128)(2,1)} %refs_0_.3), channel_id=1, source_target_pairs={{0,1},{1,0},{2,3},{3,2},{4,5},{5,4},{6,7},{7,6},{8,9},{9,8},{10,11... | collective-permute-start | bytes 3145736 | tf_op jit(solution)/shard_map/ppermute | solution.py:36
  60.9 11.8 %collective-permute-start.12 = (bf16[256,384]{1,0:T(8,128)(2,1)S(1)}, bf16[256,384]{1,0:T(8,128)(2,1)S(1)}, u32[]{:S(2)}, u32[]{:S(2)}) collective-permute-start(bf16[256,384]{1,0:T(8,128)(2,1)S(1)} %get-tuple-element.71), channel_id=1, source_target_pairs={{0,8},{8,0},{16,24},{24,16},{1,9},{9,1},{17,25},{25,17},{2,10},{10... | collective-permute-start | bytes 589832 | tf_op jit(solution)/shard_map/ppermute | solution.py:61
  70.7 15.7 %collective-permute-start.16 = (bf16[256,512]{1,0:T(8,128)(2,1)}, bf16[256,512]{1,0:T(8,128)(2,1)S(1)}, u32[]{:S(2)}, u32[]{:S(2)}) collective-permute-start(bf16[256,512]{1,0:T(8,128)(2,1)} %constant_dynamic-slice_fusion), channel_id=1, source_target_pairs={{0,6},{1,7},{2,4},{3,5},{4,2},{5,3},{6,0},{7,1},{8,14},{9,15},{10,... | collective-permute-start | bytes 786440 | tf_op jit(solution)/shard_map/ppermute | solution.py:56
  96.8 16.4 %collective-permute-start.21 = (bf16[384,512]{1,0:T(8,128)(2,1)}, bf16[384,512]{1,0:T(8,128)(2,1)S(1)}, u32[]{:S(2)}, u32[]{:S(2)}) collective-permute-start(bf16[384,512]{1,0:T(8,128)(2,1)} %get-tuple-element.97.refs_1_), channel_id=1, source_target_pairs={{0,8},{8,0},{16,24},{24,16},{1,9},{9,1},{17,25},{25,17},{2,10},{10... | collective-permute-start | bytes 1179656 | tf_op jit(solution)/shard_map/ppermute | solution.py:61
  97.8 16.5 %collective-permute-start.23 = (bf16[384,512]{1,0:T(8,128)(2,1)}, bf16[384,512]{1,0:T(8,128)(2,1)S(1)}, u32[]{:S(2)}, u32[]{:S(2)}) collective-permute-start(bf16[384,512]{1,0:T(8,128)(2,1)} %get-tuple-element.97.refs_1_), channel_id=1, source_target_pairs={{0,16},{8,24},{16,0},{24,8},{1,17},{9,25},{17,1},{25,9},{2,18},{10... | collective-permute-start | bytes 1179656 | tf_op jit(solution)/shard_map/ppermute | solution.py:61
  98.7 15.6 %collective-permute-start.22 = (bf16[384,512]{1,0:T(8,128)(2,1)}, bf16[384,512]{1,0:T(8,128)(2,1)S(1)}, u32[]{:S(2)}, u32[]{:S(2)}) collective-permute-start(bf16[384,512]{1,0:T(8,128)(2,1)} %get-tuple-element.98.refs_2_), channel_id=1, source_target_pairs={{0,8},{8,0},{16,24},{24,16},{1,9},{9,1},{17,25},{25,17},{2,10},{10... | collective-permute-start | bytes 1179656 | tf_op jit(solution)/shard_map/ppermute | solution.py:61
  100.2 14.6 %collective-permute-start.24 = (bf16[384,512]{1,0:T(8,128)(2,1)}, bf16[384,512]{1,0:T(8,128)(2,1)S(1)}, u32[]{:S(2)}, u32[]{:S(2)}) collective-permute-start(bf16[384,512]{1,0:T(8,128)(2,1)} %get-tuple-element.98.refs_2_), channel_id=1, source_target_pairs={{0,16},{8,24},{16,0},{24,8},{1,17},{9,25},{17,1},{25,9},{2,18},{10... | collective-permute-start | bytes 1179656 | tf_op jit(solution)/shard_map/ppermute | solution.py:61
  109.9 22.6 %all-to-all-start = ((bf16[32,64,128]{2,1,0:T(8,128)(2,1)}), bf16[32,64,128]{2,1,0:T(8,128)(2,1)S(1)}, u32[]{:S(2)}, u32[]{:S(2)}) async-start(bf16[32,64,128]{2,1,0:T(8,128)(2,1)} %bitcast.34), calls=%async_computation | async-start | bytes 1048576 | tf_op jit(solution)/shard_map/all_to_all | solution.py:364
  114.8 15.2 %collective-permute-start.25 = (bf16[384,512]{1,0:T(8,128)(2,1)S(1)}, bf16[384,512]{1,0:T(8,128)(2,1)}, u32[]{:S(2)}, u32[]{:S(2)}) collective-permute-start(bf16[384,512]{1,0:T(8,128)(2,1)S(1)} %collective-permute-done.23.refs_5_), channel_id=1, source_target_pairs={{0,8},{8,0},{16,24},{24,16},{1,9},{9,1},{17,25},{25,17},{2,10},{10... | collective-permute-start | bytes 1179656 | tf_op jit(solution)/shard_map/ppermute | solution.py:61
  116.0 14.5 %collective-permute-start.26 = (bf16[384,512]{1,0:T(8,128)(2,1)S(1)}, bf16[384,512]{1,0:T(8,128)(2,1)}, u32[]{:S(2)}, u32[]{:S(2)}) collective-permute-start(bf16[384,512]{1,0:T(8,128)(2,1)S(1)} %collective-permute-done.22.refs_4_), channel_id=1, source_target_pairs={{0,16},{8,24},{16,0},{24,8},{1,17},{9,25},{17,1},{25,9},{2,18},{10... | collective-permute-start | bytes 1179656 | tf_op jit(solution)/shard_map/ppermute | solution.py:61
  117.0 13.6 %collective-permute-start.30 = (bf16[384,512]{1,0:T(8,128)(2,1)S(1)}, bf16[384,512]{1,0:T(8,128)(2,1)S(1)}, u32[]{:S(2)}, u32[]{:S(2)}) collective-permute-start(bf16[384,512]{1,0:T(8,128)(2,1)S(1)} %collective-permute-done.21.refs_3_), channel_id=1, source_target_pairs={{0,1},{1,0},{2,3},{3,2},{4,5},{5,4},{6,7},{7,6},{8,9},{9,8},{10,11... | collective-permute-start | bytes 1179656 | tf_op jit(solution)/shard_map/ppermute | solution.py:36
  117.0 15.5 %collective-permute-start.31 = (bf16[384,512]{1,0:T(8,128)(2,1)S(1)}, bf16[384,512]{1,0:T(8,128)(2,1)S(1)}, u32[]{:S(2)}, u32[]{:S(2)}) collective-permute-start(bf16[384,512]{1,0:T(8,128)(2,1)S(1)} %collective-permute-done.22.refs_4_), channel_id=1, source_target_pairs={{0,1},{1,0},{2,3},{3,2},{4,5},{5,4},{6,7},{7,6},{8,9},{9,8},{10,11... | collective-permute-start | bytes 1179656 | tf_op jit(solution)/shard_map/ppermute | solution.py:36
  117.5 15.0 %collective-permute-start.32 = (bf16[384,512]{1,0:T(8,128)(2,1)S(1)}, bf16[384,512]{1,0:T(8,128)(2,1)S(1)}, u32[]{:S(2)}, u32[]{:S(2)}) collective-permute-start(bf16[384,512]{1,0:T(8,128)(2,1)S(1)} %collective-permute-done.23.refs_5_), channel_id=1, source_target_pairs={{0,1},{1,0},{2,3},{3,2},{4,5},{5,4},{6,7},{7,6},{8,9},{9,8},{10,11... | collective-permute-start | bytes 1179656 | tf_op jit(solution)/shard_map/ppermute | solution.py:36
  184.3 30.4 %all-to-all-start.2 = ((bf16[32,8,2048]{2,1,0:T(8,128)(2,1)}), bf16[32,8,2048]{2,1,0:T(8,128)(2,1)S(1)}, u32[]{:S(2)}, u32[]{:S(2)}) async-start(bf16[32,8,2048]{2,1,0:T(8,128)(2,1)} %bitcast.28), calls=%async_computation.2 | async-start | bytes 2097152 | tf_op jit(solution)/shard_map/all_to_all | solution.py:393
  (43 other events, 453.3 us)

commit v4 on v3

--- a/solution.py
+++ b/solution.py
@@ -163,13 +163,19 @@
     mine = spot // 2
     block, quarter = joined.shape[0] // 2, weights[0][1].shape[1]
     pair = 2 * DH
+    depth = (planes - 1) * DH
+    side_width = planes * pair
     for source in range(4):
         rows = pl.ds(pl.multiple_of((source // 2 ^ mine) * block, block), block)
-        for head in range(2 * planes):
-            columns = pl.ds(head * pair + source % 2 * DH, DH)
-            joined[rows, columns] = heads_ref[
-                pl.ds((source * 2 * planes + head) * block, block), :
-            ]
+        half = source % 2
+        for side in range(2):
+            for offset in range(planes):
+                device = 2 * (place ^ offset) + (core ^ side)
+                start = pl.multiple_of((source * 2 * planes + device) * block, block)
+                inner = half * DH if offset == 0 else pair + half * depth + (offset - 1) * DH
+                joined[rows, pl.ds(side * side_width + inner, DH)] = heads_ref[
+                    pl.ds(start, block), :
+                ]
     joined[...] = jnp.where(live_ref[...] > 0, joined[...].astype(jnp.float32), 0.0).astype(
         jnp.bfloat16
     )
@@ -178,22 +184,17 @@
         columns = pl.ds(pl.multiple_of((spot ^ bits) * quarter, quarter), quarter)
         total = own_ref[:, columns].astype(jnp.float32)
         for side in range(2):
-            for offset in range(planes):
-                device = 2 * (place ^ offset) + (core ^ side)
-                start = pl.multiple_of(device * pair, pair)
-                if offset == 0:
-                    total += jnp.dot(
-                        joined[:, pl.ds(start, pair)],
-                        weights[side][0][:, columns],
-                        preferred_element_type=jnp.float32,
-                    )
-                    continue
-                for half in range(2):
-                    total += jnp.dot(
-                        joined[:, pl.ds(start + half * DH, DH)],
-                        weights[side][1 + 2 * bits + half][pl.ds((offset - 1) * DH, DH), :],
-                        preferred_element_type=jnp.float32,
-                    )
+            total += jnp.dot(
+                joined[:, pl.ds(side * side_width, pair)],
+                weights[side][0][:, columns],
+                preferred_element_type=jnp.float32,
+            )
+            for half in range(2):
+                total += jnp.dot(
+                    joined[:, pl.ds(side * side_width + pair + half * depth, depth)],
+                    weights[side][1 + 2 * bits + half][...],
+                    preferred_element_type=jnp.float32,
+                )
         residual_ref[:, columns] = total
         squares += jnp.sum(total * total, axis=1, keepdims=True)
     residual = residual_ref[...]

time: 217 us -> 217 us (level)
  transfers between devices with their start and end apart: 38 -> 38, of which waited for: 15 -> 15; matrix products, arithmetic and copies ran while one was open for 6% -> 6% of each run, Pallas kernels for 8% -> 9%
where the time goes in v4:
time: 217 us; the launch traced here: 216 us
  waiting for transfers between devices  94.2 us (43%)
  Pallas kernels  38.4 us (18%)
  starting transfers between devices  36.7 us (17%)
  blocking collectives  32 us (15%)
  local copies, waits for them, and re-layouts  10.6 us (5%)
  other arithmetic  3.74 us (2%)
    pallas_call x7, Pallas kernels, local_call(): pl.pallas_call(body, out_shape=outs, in_specs=specs, out_specs=[VMEM] * l...  36 us
    all_to_all x1, blocking collectives, paired_shards(): received = lax.all_to_all(send_rows, everyone, 0, 0, tiled=True)  32 us
    all_to_all x1, waiting for transfers between devices, paired_shards(): gathered = lax.all_to_all(computed, everyone, 0, 0, tiled=True)  27.5 us
    ppermute x12, waiting for transfers between devices, in_plane(): return lax.ppermute(block, 'expert', [(e, e ^ bits) for e in range(count)])  27.3 us
    ppermute x2, waiting for transfers between devices, outwards(): return lax.ppermute(block, 'head', route)  22.3 us
    ppermute x12, starting transfers between devices, in_plane(): return lax.ppermute(block, 'expert', [(e, e ^ bits) for e in range(count)])  14.2 us
    ppermute x3, waiting for transfers between devices, across_z(): lax.ppermute(block, 'head', [(h, h ^ 2 * bits) for h in range(count)])  12 us
    ppermute x3, starting transfers between devices, neighbours(): return lax.ppermute(block, 'head', route)  7.61 us
  transfers between devices with their start and end apart: 38, of which 15 were waited for; matrix products, arithmetic and copies ran while one was open for 6% of the time, Pallas kernels for 9%

profile of v4, /device:TPU:0, one launch (start us, length us, event | category | flops | bytes accessed | tf_op | source)
XLA Modules:
  0.0 216.0 jit_solution(10349433859556874969)
XLA Ops:
  0.5 2.1 fusion.1
  5.4 4.7 %collective-permute-start.4 = (bf16[128,2048]{1,0:T(8,128)(2,1)}, bf16[128,2048]{1,0:T(8,128)(2,1)}, u32[]{:S(2)}, u32[]{:S(2)}) collective-permute-start(bf16[128,2048]{1,0:T(8,128)(2,1)} %maximum_select_fusion.refs_0_.own_ref), channel_id=1, source_target_pairs={{0,2},{2,0},{1,3},{3,1},{4,6},{6,4},{5,7},{7,5},{8,10},{10,8},{9,1... | collective-permute-start | bytes 1572872 | tf_op jit(solution)/shard_map/ppermute | solution.py:46
  16.2 2.4 %shard_map.118.refs_4_ = bf16[2048,768]{1,0:T(8,128)(2,1)S(1)} custom-call(s32[1]{0:T(128)} %bitcast.13.place_ref, bf16[2048,256]{1,0:T(8,128)(2,1)} %refs_0_.2, bf16[2048,256]{1,0:T(8,128)(2,1)} %refs_1_.1, bf16[2048,256]{1,0:T(8,128)(2,1)} %refs_2_.1), custom_call_target="tpu_custom_call" | custom-call | bytes 12582912 | tf_op jit(solution)/shard_map/pallas_call | solution.py:280
  19.2 3.9 %collective-permute-done.4.refs_2_ = bf16[128,2048]{1,0:T(8,128)(2,1)} collective-permute-done((bf16[128,2048]{1,0:T(8,128)(2,1)}, bf16[128,2048]{1,0:T(8,128)(2,1)}, u32[]{:S(2)}, u32[]{:S(2)}) %collective-permute-start.4) | collective-permute-done | bytes 524320 | tf_op jit(solution)/shard_map/ppermute | solution.py:46
  24.5 3.6 %collective-permute-done.2.refs_0_ = bf16[256,512]{1,0:T(8,128)(2,1)S(1)} collective-permute-done((bf16[256,512]{1,0:T(8,128)(2,1)}, bf16[256,512]{1,0:T(8,128)(2,1)S(1)}, u32[]{:S(2)}, u32[]{:S(2)}) %collective-permute-start.2) | collective-permute-done | bytes 262176 | tf_op jit(solution)/shard_map/ppermute | solution.py:56
  31.1 14.2 %collective-permute-done.3 = bf16[128,2048]{1,0:T(8,128)(2,1)} collective-permute-done((bf16[128,2048]{1,0:T(8,128)(2,1)}, bf16[128,2048]{1,0:T(8,128)(2,1)}, u32[]{:S(2)}, u32[]{:S(2)}) %collective-permute-start.3) | collective-permute-done | bytes 524320 | tf_op jit(solution)/shard_map/ppermute | solution.py:51
  46.9 8.2 %collective-permute-done.6 = bf16[128,2048]{1,0:T(8,128)(2,1)S(1)} collective-permute-done((bf16[128,2048]{1,0:T(8,128)(2,1)}, bf16[128,2048]{1,0:T(8,128)(2,1)S(1)}, u32[]{:S(2)}, u32[]{:S(2)}) %collective-permute-start.6) | collective-permute-done | bytes 524320 | tf_op jit(solution)/shard_map/ppermute | solution.py:51
  57.2 3.0 %shard_map.120 = (bf16[256,384]{1,0:T(8,128)(2,1)S(1)}, bf16[256,384]{1,0:T(8,128)(2,1)S(1)}, bf16[256,384]{1,0:T(8,128)(2,1)S(1)}, bf16[256,384]{1,0:T(8,128)(2,1)S(1)}) custom-call(bf16[128,2048]{1,0:T(8,128)(2,1)} %maximum_select_fusion.refs_0_.own_ref, bf16[128,2048]{1,0:T(8,128)(2,1)S(1)} %collective-permute-done.10.refs_1_, ...), custom_call_target="tpu_custom_call" | custom-call | flops 1610612736 | bytes 6029312 | tf_op jit(solution)/shard_map/pallas_call | solution.py:19
  62.3 8.4 %collective-permute-done.15.refs_1_ = bf16[256,512]{1,0:T(8,128)(2,1)S(1)} collective-permute-done((bf16[256,512]{1,0:T(8,128)(2,1)}, bf16[256,512]{1,0:T(8,128)(2,1)S(1)}, u32[]{:S(2)}, u32[]{:S(2)}) %collective-permute-start.15) | collective-permute-done | bytes 262176 | tf_op jit(solution)/shard_map/ppermute | solution.py:56
  70.7 2.0 collective-permute-start.16
  75.6 1.8 shard_map.119
  78.1 5.2 %collective-permute-done.13.refs_2_ = bf16[256,384]{1,0:T(8,128)(2,1)S(1)} collective-permute-done((bf16[256,384]{1,0:T(8,128)(2,1)S(1)}, bf16[256,384]{1,0:T(8,128)(2,1)S(1)}, u32[]{:S(2)}, u32[]{:S(2)}) %collective-permute-start.13) | collective-permute-done | bytes 196640 | tf_op jit(solution)/shard_map/ppermute | solution.py:61
  86.9 4.1 %collective-permute-done.17.refs_5_ = bf16[256,384]{1,0:T(8,128)(2,1)S(1)} collective-permute-done((bf16[256,384]{1,0:T(8,128)(2,1)S(1)}, bf16[256,384]{1,0:T(8,128)(2,1)S(1)}, u32[]{:S(2)}, u32[]{:S(2)}) %collective-permute-start.17) | collective-permute-done | bytes 196640 | tf_op jit(solution)/shard_map/ppermute | solution.py:61
  91.0 3.6 %collective-permute-done.18.refs_6_ = bf16[256,384]{1,0:T(8,128)(2,1)S(1)} collective-permute-done((bf16[256,384]{1,0:T(8,128)(2,1)S(1)}, bf16[256,384]{1,0:T(8,128)(2,1)S(1)}, u32[]{:S(2)}, u32[]{:S(2)}) %collective-permute-start.18) | collective-permute-done | bytes 196640 | tf_op jit(solution)/shard_map/ppermute | solution.py:61
  94.7 2.2 %shard_map.121 = (bf16[384,512]{1,0:T(8,128)(2,1)}, bf16[384,512]{1,0:T(8,128)(2,1)}) custom-call(bf16[256,512]{1,0:T(8,128)(2,1)} %copy-done.17, bf16[256,512]{1,0:T(8,128)(2,1)} %copy-done.18, bf16[256,512]{1,0:T(8,128)(2,1)} %copy-done.19), custom_call_target="tpu_custom_call" | custom-call | bytes 1572864 | tf_op jit(solution)/shard_map/pallas_call | solution.py:19
  100.9 9.1 %shard_map.122 = bf16[2048,128]{1,0:T(8,128)(2,1)} custom-call(s32[3]{0:T(128)} %pad_add_fusion.place_ref, f32[1,2048]{1,0:T(1,128)} %select_n.91.bias_ref, bf16[256,384]{1,0:T(8,128)(2,1)} %copy-done.2, bf16[256,384]{1,0:T(8,128)(2,1)} %copy-done.23, bf16[256,384]{1,0:T(8,128)(2,1)} %copy-done.24, bf16[256,384]{1,0:T(8,128)(2,1)} %copy-done.25, ...), custom_call_target="tpu_custom_call" | custom-call | flops 2147483648 | bytes 2105356 | tf_op jit(solution)/shard_map/pallas_call | solution.py:19
  109.9 3.2 %all-to-all-start = ((bf16[32,64,128]{2,1,0:T(8,128)(2,1)}), bf16[32,64,128]{2,1,0:T(8,128)(2,1)S(1)}, u32[]{:S(2)}, u32[]{:S(2)}) async-start(bf16[32,64,128]{2,1,0:T(8,128)(2,1)} %bitcast.34), calls=%async_computation | async-start | bytes 1048576 | tf_op jit(solution)/shard_map/all_to_all | solution.py:365
  117.6 12.4 %collective-permute-done.25.refs_7_ = bf16[384,512]{1,0:T(8,128)(2,1)} collective-permute-done((bf16[384,512]{1,0:T(8,128)(2,1)S(1)}, bf16[384,512]{1,0:T(8,128)(2,1)}, u32[]{:S(2)}, u32[]{:S(2)}) %collective-permute-start.25) | collective-permute-done | bytes 393248 | tf_op jit(solution)/shard_map/ppermute | solution.py:61
  133.6 6.9 %shard_map.123 = (f32[128,2048]{1,0:T(8,128)}, bf16[256,2048]{1,0:T(8,128)(2,1)}) custom-call(s32[3]{0:T(128)} %pad_add_fusion.place_ref, bf16[128,2048]{1,0:T(8,128)(2,1)} %maximum_select_fusion.refs_0_.own_ref, s32[128,1]{1,0:T(8,128)} %copy.19.live_ref, s32[1,128]{1,0:T(1,128)} %reshape.254.target_ref, bf16[1,2048]{1,0:T(2,128)(2,1)} %reshape.255.gain_ref, ...), custom_call_target="tpu_custom_call" | custom-call | flops 1207959552 | bytes 11539468 | tf_op jit(solution)/shard_map/pallas_call | solution.py:19
  140.6 32.0 %all_to_all.33 = bf16[32,8,2048]{2,1,0:T(8,128)(2,1)} all-to-all(bf16[32,8,2048]{2,1,0:T(8,128)(2,1)} %bitcast.33), channel_id=1, replica_groups=mesh['expert'=4,'head'=8] {'expert','head'}, dimensions={0} | all-to-all | bytes 2097152 | tf_op jit(solution)/shard_map/all_to_all | solution.py:384
  172.6 11.2 %shard_map.124 = bf16[256,2048]{1,0:T(8,128)(2,1)} custom-call(bf16[256,2048]{1,0:T(8,128)(2,1)} %bitcast.29, bf16[704,2048]{1,0:T(8,128)(2,1)} %bitcast.31, bf16[704,2048]{1,0:T(8,128)(2,1)} %bitcast.15.refs_1_, bf16[704,2048]{1,0:T(8,128)(2,1)} %bitcast.16.refs_2_, bf16[704,2048]{1,0:T(8,128)(2,1)} %collective-permute-done.1.refs_3_, ...), custom_call_target="tpu_custom_call" | custom-call | flops 4429185024 | bytes 19398656 | tf_op jit(solution)/shard_map/pallas_call | solution.py:19
  183.8 2.8 %all-to-all-start.2 = ((bf16[32,8,2048]{2,1,0:T(8,128)(2,1)}), bf16[32,8,2048]{2,1,0:T(8,128)(2,1)S(1)}, u32[]{:S(2)}, u32[]{:S(2)}) async-start(bf16[32,8,2048]{2,1,0:T(8,128)(2,1)} %bitcast.28), calls=%async_computation.2 | async-start | bytes 2097152 | tf_op jit(solution)/shard_map/all_to_all | solution.py:394
  186.7 27.5 %all-to-all-done.2 = bf16[32,8,2048]{2,1,0:T(8,128)(2,1)S(1)} async-done(((bf16[32,8,2048]{2,1,0:T(8,128)(2,1)}), bf16[32,8,2048]{2,1,0:T(8,128)(2,1)S(1)}, u32[]{:S(2)}, u32[]{:S(2)}) %all-to-all-start.2) | async-done | bytes 1048608 | tf_op jit(solution)/shard_map/all_to_all | solution.py:394
  214.2 1.8 shard_map.125
  (147 shorter events, 39.5 us)
Async XLA Ops:
  0.0 28.2 %collective-permute-start.1 = (bf16[704,2048]{1,0:T(8,128)(2,1)}, bf16[704,2048]{1,0:T(8,128)(2,1)}, u32[]{:S(2)}, u32[]{:S(2)}) collective-permute-start(bf16[704,2048]{1,0:T(8,128)(2,1)} %bitcast.30), channel_id=1, source_target_pairs={{0,1},{1,0},{2,3},{3,2},{4,5},{5,4},{6,7},{7,6},{8,9},{9,8},{10,11... | collective-permute-start | bytes 8650760 | tf_op jit(solution)/shard_map/ppermute | solution.py:36
  3.9 24.3 %collective-permute-start = (bf16[128,2048]{1,0:T(8,128)(2,1)}, bf16[128,2048]{1,0:T(8,128)(2,1)}, u32[]{:S(2)}, u32[]{:S(2)}) collective-permute-start(bf16[128,2048]{1,0:T(8,128)(2,1)} %maximum_select_fusion.refs_0_.own_ref), channel_id=1, source_target_pairs={{2,4},{4,2},{3,5},{5,3},{10,12},{12,10},{11,13},{13,11},{18,20},{2... | collective-permute-start | bytes 1572872 | tf_op jit(solution)/shard_map/ppermute | solution.py:46
  5.4 17.7 %collective-permute-start.4 = (bf16[128,2048]{1,0:T(8,128)(2,1)}, bf16[128,2048]{1,0:T(8,128)(2,1)}, u32[]{:S(2)}, u32[]{:S(2)}) collective-permute-start(bf16[128,2048]{1,0:T(8,128)(2,1)} %maximum_select_fusion.refs_0_.own_ref), channel_id=1, source_target_pairs={{0,2},{2,0},{1,3},{3,1},{4,6},{6,4},{5,7},{7,5},{8,10},{10,8},{9,1... | collective-permute-start | bytes 1572872 | tf_op jit(solution)/shard_map/ppermute | solution.py:46
  11.7 16.5 %collective-permute-start.2 = (bf16[256,512]{1,0:T(8,128)(2,1)}, bf16[256,512]{1,0:T(8,128)(2,1)S(1)}, u32[]{:S(2)}, u32[]{:S(2)}) collective-permute-start(bf16[256,512]{1,0:T(8,128)(2,1)} %constant_dynamic-slice_fusion), channel_id=1, source_target_pairs={{0,2},{1,3},{2,0},{3,1},{4,6},{5,7},{6,4},{7,5},{8,10},{9,11},{10,... | collective-permute-start | bytes 786440 | tf_op jit(solution)/shard_map/ppermute | solution.py:56
  11.7 43.3 %collective-permute-start.8 = (bf16[704,2048]{1,0:T(8,128)(2,1)}, bf16[704,2048]{1,0:T(8,128)(2,1)}, u32[]{:S(2)}, u32[]{:S(2)}) collective-permute-start(bf16[704,2048]{1,0:T(8,128)(2,1)} %bitcast.15.refs_1_), channel_id=1, source_target_pairs={{0,1},{1,0},{2,3},{3,2},{4,5},{5,4},{6,7},{7,6},{8,9},{9,8},{10,11... | collective-permute-start | bytes 8650760 | tf_op jit(solution)/shard_map/ppermute | solution.py:36
  28.2 17.0 %collective-permute-start.3 = (bf16[128,2048]{1,0:T(8,128)(2,1)}, bf16[128,2048]{1,0:T(8,128)(2,1)}, u32[]{:S(2)}, u32[]{:S(2)}) collective-permute-start(bf16[128,2048]{1,0:T(8,128)(2,1)} %collective-permute-done), channel_id=1, source_target_pairs={{2,0},{3,1},{4,6},{5,7},{10,8},{11,9},{12,14},{13,15},{18,16},{19,... | collective-permute-start | bytes 1572872 | tf_op jit(solution)/shard_map/ppermute | solution.py:51
  29.5 57.4 %collective-permute-start.20 = (bf16[704,2048]{1,0:T(8,128)(2,1)}, bf16[704,2048]{1,0:T(8,128)(2,1)}, u32[]{:S(2)}, u32[]{:S(2)}) collective-permute-start(bf16[704,2048]{1,0:T(8,128)(2,1)} %bitcast.16.refs_2_), channel_id=1, source_target_pairs={{0,1},{1,0},{2,3},{3,2},{4,5},{5,4},{6,7},{7,6},{8,9},{9,8},{10,11... | collective-permute-start | bytes 8650760 | tf_op jit(solution)/shard_map/ppermute | solution.py:36
  29.6 25.5 %collective-permute-start.6 = (bf16[128,2048]{1,0:T(8,128)(2,1)}, bf16[128,2048]{1,0:T(8,128)(2,1)S(1)}, u32[]{:S(2)}, u32[]{:S(2)}) collective-permute-start(bf16[128,2048]{1,0:T(8,128)(2,1)} %collective-permute-done.5), channel_id=1, source_target_pairs={{2,0},{3,1},{4,6},{5,7},{10,8},{11,9},{12,14},{13,15},{18,16},{19,... | collective-permute-start | bytes 1572872 | tf_op jit(solution)/shard_map/ppermute | solution.py:51
  55.1 19.1 %collective-permute-start.9 = (bf16[128,2048]{1,0:T(8,128)(2,1)S(1)}, bf16[128,2048]{1,0:T(8,128)(2,1)S(1)}, u32[]{:S(2)}, u32[]{:S(2)}) collective-permute-start(bf16[128,2048]{1,0:T(8,128)(2,1)S(1)} %broadcast_select_fusion.refs_2_), channel_id=1, source_target_pairs={{0,1},{1,0},{2,3},{3,2},{4,5},{5,4},{6,7},{7,6},{8,9},{9,8},{10,11... | collective-permute-start | bytes 1572872 | tf_op jit(solution)/shard_map/ppermute | solution.py:36
  55.7 15.0 %collective-permute-start.15 = (bf16[256,512]{1,0:T(8,128)(2,1)}, bf16[256,512]{1,0:T(8,128)(2,1)S(1)}, u32[]{:S(2)}, u32[]{:S(2)}) collective-permute-start(bf16[256,512]{1,0:T(8,128)(2,1)} %constant_dynamic-slice_fusion), channel_id=1, source_target_pairs={{0,4},{1,5},{2,6},{3,7},{4,0},{5,1},{6,2},{7,3},{8,12},{9,13},{10,... | collective-permute-start | bytes 786440 | tf_op jit(solution)/shard_map/ppermute | solution.py:56
  56.9 60.1 %collective-permute-start.27 = (bf16[256,2048]{1,0:T(8,128)(2,1)}, bf16[256,2048]{1,0:T(8,128)(2,1)}, u32[]{:S(2)}, u32[]{:S(2)}) collective-permute-start(bf16[256,2048]{1,0:T(8,128)(2,1)} %refs_0_.3), channel_id=1, source_target_pairs={{0,1},{1,0},{2,3},{3,2},{4,5},{5,4},{6,7},{7,6},{8,9},{9,8},{10,11... | collective-permute-start | bytes 3145736 | tf_op jit(solution)/shard_map/ppermute | solution.py:36
  60.9 11.8 %collective-permute-start.12 = (bf16[256,384]{1,0:T(8,128)(2,1)S(1)}, bf16[256,384]{1,0:T(8,128)(2,1)S(1)}, u32[]{:S(2)}, u32[]{:S(2)}) collective-permute-start(bf16[256,384]{1,0:T(8,128)(2,1)S(1)} %get-tuple-element.71), channel_id=1, source_target_pairs={{0,8},{8,0},{16,24},{24,16},{1,9},{9,1},{17,25},{25,17},{2,10},{10... | collective-permute-start | bytes 589832 | tf_op jit(solution)/shard_map/ppermute | solution.py:61
  70.7 15.7 %collective-permute-start.16 = (bf16[256,512]{1,0:T(8,128)(2,1)}, bf16[256,512]{1,0:T(8,128)(2,1)S(1)}, u32[]{:S(2)}, u32[]{:S(2)}) collective-permute-start(bf16[256,512]{1,0:T(8,128)(2,1)} %constant_dynamic-slice_fusion), channel_id=1, source_target_pairs={{0,6},{1,7},{2,4},{3,5},{4,2},{5,3},{6,0},{7,1},{8,14},{9,15},{10,... | collective-permute-start | bytes 786440 | tf_op jit(solution)/shard_map/ppermute | solution.py:56
  96.8 16.4 %collective-permute-start.21 = (bf16[384,512]{1,0:T(8,128)(2,1)}, bf16[384,512]{1,0:T(8,128)(2,1)S(1)}, u32[]{:S(2)}, u32[]{:S(2)}) collective-permute-start(bf16[384,512]{1,0:T(8,128)(2,1)} %get-tuple-element.97.refs_1_), channel_id=1, source_target_pairs={{0,8},{8,0},{16,24},{24,16},{1,9},{9,1},{17,25},{25,17},{2,10},{10... | collective-permute-start | bytes 1179656 | tf_op jit(solution)/shard_map/ppermute | solution.py:61
  97.8 16.5 %collective-permute-start.23 = (bf16[384,512]{1,0:T(8,128)(2,1)}, bf16[384,512]{1,0:T(8,128)(2,1)S(1)}, u32[]{:S(2)}, u32[]{:S(2)}) collective-permute-start(bf16[384,512]{1,0:T(8,128)(2,1)} %get-tuple-element.97.refs_1_), channel_id=1, source_target_pairs={{0,16},{8,24},{16,0},{24,8},{1,17},{9,25},{17,1},{25,9},{2,18},{10... | collective-permute-start | bytes 1179656 | tf_op jit(solution)/shard_map/ppermute | solution.py:61
  98.7 15.6 %collective-permute-start.22 = (bf16[384,512]{1,0:T(8,128)(2,1)}, bf16[384,512]{1,0:T(8,128)(2,1)S(1)}, u32[]{:S(2)}, u32[]{:S(2)}) collective-permute-start(bf16[384,512]{1,0:T(8,128)(2,1)} %get-tuple-element.98.refs_2_), channel_id=1, source_target_pairs={{0,8},{8,0},{16,24},{24,16},{1,9},{9,1},{17,25},{25,17},{2,10},{10... | collective-permute-start | bytes 1179656 | tf_op jit(solution)/shard_map/ppermute | solution.py:61
  100.2 14.6 %collective-permute-start.24 = (bf16[384,512]{1,0:T(8,128)(2,1)}, bf16[384,512]{1,0:T(8,128)(2,1)S(1)}, u32[]{:S(2)}, u32[]{:S(2)}) collective-permute-start(bf16[384,512]{1,0:T(8,128)(2,1)} %get-tuple-element.98.refs_2_), channel_id=1, source_target_pairs={{0,16},{8,24},{16,0},{24,8},{1,17},{9,25},{17,1},{25,9},{2,18},{10... | collective-permute-start | bytes 1179656 | tf_op jit(solution)/shard_map/ppermute | solution.py:61
  109.9 22.6 %all-to-all-start = ((bf16[32,64,128]{2,1,0:T(8,128)(2,1)}), bf16[32,64,128]{2,1,0:T(8,128)(2,1)S(1)}, u32[]{:S(2)}, u32[]{:S(2)}) async-start(bf16[32,64,128]{2,1,0:T(8,128)(2,1)} %bitcast.34), calls=%async_computation | async-start | bytes 1048576 | tf_op jit(solution)/shard_map/all_to_all | solution.py:365
  114.8 15.2 %collective-permute-start.25 = (bf16[384,512]{1,0:T(8,128)(2,1)S(1)}, bf16[384,512]{1,0:T(8,128)(2,1)}, u32[]{:S(2)}, u32[]{:S(2)}) collective-permute-start(bf16[384,512]{1,0:T(8,128)(2,1)S(1)} %collective-permute-done.23.refs_5_), channel_id=1, source_target_pairs={{0,8},{8,0},{16,24},{24,16},{1,9},{9,1},{17,25},{25,17},{2,10},{10... | collective-permute-start | bytes 1179656 | tf_op jit(solution)/shard_map/ppermute | solution.py:61
  116.0 14.5 %collective-permute-start.26 = (bf16[384,512]{1,0:T(8,128)(2,1)S(1)}, bf16[384,512]{1,0:T(8,128)(2,1)}, u32[]{:S(2)}, u32[]{:S(2)}) collective-permute-start(bf16[384,512]{1,0:T(8,128)(2,1)S(1)} %collective-permute-done.22.refs_4_), channel_id=1, source_target_pairs={{0,16},{8,24},{16,0},{24,8},{1,17},{9,25},{17,1},{25,9},{2,18},{10... | collective-permute-start | bytes 1179656 | tf_op jit(solution)/shard_map/ppermute | solution.py:61
  117.0 13.6 %collective-permute-start.30 = (bf16[384,512]{1,0:T(8,128)(2,1)S(1)}, bf16[384,512]{1,0:T(8,128)(2,1)S(1)}, u32[]{:S(2)}, u32[]{:S(2)}) collective-permute-start(bf16[384,512]{1,0:T(8,128)(2,1)S(1)} %collective-permute-done.21.refs_3_), channel_id=1, source_target_pairs={{0,1},{1,0},{2,3},{3,2},{4,5},{5,4},{6,7},{7,6},{8,9},{9,8},{10,11... | collective-permute-start | bytes 1179656 | tf_op jit(solution)/shard_map/ppermute | solution.py:36
  117.0 15.5 %collective-permute-start.31 = (bf16[384,512]{1,0:T(8,128)(2,1)S(1)}, bf16[384,512]{1,0:T(8,128)(2,1)S(1)}, u32[]{:S(2)}, u32[]{:S(2)}) collective-permute-start(bf16[384,512]{1,0:T(8,128)(2,1)S(1)} %collective-permute-done.22.refs_4_), channel_id=1, source_target_pairs={{0,1},{1,0},{2,3},{3,2},{4,5},{5,4},{6,7},{7,6},{8,9},{9,8},{10,11... | collective-permute-start | bytes 1179656 | tf_op jit(solution)/shard_map/ppermute | solution.py:36
  117.5 15.0 %collective-permute-start.32 = (bf16[384,512]{1,0:T(8,128)(2,1)S(1)}, bf16[384,512]{1,0:T(8,128)(2,1)S(1)}, u32[]{:S(2)}, u32[]{:S(2)}) collective-permute-start(bf16[384,512]{1,0:T(8,128)(2,1)S(1)} %collective-permute-done.23.refs_5_), channel_id=1, source_target_pairs={{0,1},{1,0},{2,3},{3,2},{4,5},{5,4},{6,7},{7,6},{8,9},{9,8},{10,11... | collective-permute-start | bytes 1179656 | tf_op jit(solution)/shard_map/ppermute | solution.py:36
  183.8 30.4 %all-to-all-start.2 = ((bf16[32,8,2048]{2,1,0:T(8,128)(2,1)}), bf16[32,8,2048]{2,1,0:T(8,128)(2,1)S(1)}, u32[]{:S(2)}, u32[]{:S(2)}) async-start(bf16[32,8,2048]{2,1,0:T(8,128)(2,1)} %bitcast.28), calls=%async_computation.2 | async-start | bytes 2097152 | tf_op jit(solution)/shard_map/all_to_all | solution.py:394
  (43 other events, 453.3 us)
